TPU v7x, 128 devices: a whole 4x4x4 slice. The times are simulated.
128 devices in a mesh: row: 16 (over x, y), col: 8 (over z, core).
Axes of the slice: x: 4, y: 4, z: 4, core: 2. Of those that a mesh axis runs over, the one named last changes fastest.
Arguments:
- tile_values: float32 [40960, 128, 128], P(('row', 'col')), may hold values from 0 to 67108.87
- tile_rows: int32 [40960], P(('row', 'col')), may hold values from 0 to 127
- tile_cols: int32 [40960], P(('row', 'col')), may hold values from 0 to 255
- tile_patterns: int32 [40960], P(('row', 'col')), may hold values from 0 to 65535
- tile_counts: int32 [128], P(('row', 'col')), may hold values from 80 to 320, as said below
- factor: float32 [262144, 64], P(('row', 'col')), may hold values from 0.05 to 10, as said below
Outputs:
- factor_next: float32 [262144, 64], P(('row', 'col'))
Inputs may be any that keep to these rules, and one draw needn't show every extreme that they name: `tile_counts`: every device has at least a quarter of its slots live, and some device has all 320 live. `factor`: entries are positive.
All inputs are finite; a program needn't handle non-finite values.
Results may differ from a plain program's by a relative error of at most 0.0003.
Values sent between devices are 32-bit elements; how exact they have to be, the bound alone decides.
No kernel may reach another device: no remote copies, remote signals or barrier semaphores. Data moves between devices by JAX's collectives and lax.ppermute only.
A program may use at most 192 MiB of HBM per device.

v0:
```python
import jax
import jax.numpy as jnp
from jax import lax
from jax.sharding import PartitionSpec as P


def spread(shard, axis, root):
    mine = lax.axis_index(axis) == root
    return lax.psum(jnp.where(mine, shard, jnp.zeros_like(shard)), axis)


def expand_pattern(patterns):
    shifts = jnp.arange(16, dtype=jnp.int32)
    bits = jnp.bitwise_and(jnp.right_shift(patterns[:, None], shifts[None, :]), 1)
    return bits.reshape(-1, 4, 4).astype(jnp.float32)


def masked_tiles(values, patterns):
    sub_mask = expand_pattern(patterns)
    count_tiles = values.shape[0]
    edge = values.shape[1] // 4
    shaped = values.reshape(count_tiles, 4, edge, 4, edge) * sub_mask[:, :, None, :, None]
    return shaped.reshape(count_tiles, values.shape[1], values.shape[2])


def hals_sweep(factor, image, gram_matrix):

    def update(column, current):
        gram_col = lax.dynamic_slice_in_dim(gram_matrix, column, 1, 1)
        fitted = jnp.dot(current, gram_col, precision=lax.Precision.HIGHEST)[:, 0]
        diagonal = lax.dynamic_index_in_dim(gram_col[:, 0], column, 0, False)
        target = lax.dynamic_index_in_dim(image, column, 1, False)
        old_col = lax.dynamic_index_in_dim(current, column, 1, False)
        fresh = jnp.maximum(old_col + (target - fitted) / diagonal, 0.0)
        return lax.dynamic_update_index_in_dim(current, fresh, column, 1)

    return lax.fori_loop(0, gram_matrix.shape[0], update, factor)


def shards(tile_values, tile_rows, tile_cols, tile_patterns, tile_counts, factor):
    row_count = lax.axis_size("row")
    col_count = lax.axis_size("col")
    groups = row_count // col_count
    col_index = lax.axis_index("col")
    items_here = factor.shape[0]
    rank_width = factor.shape[1]
    tile_edge = tile_values.shape[1]
    slot_count = tile_values.shape[0]
    row_group = lax.all_gather(factor, "col", axis=0, tiled=True)
    pieces = []
    for offset in range(groups):
        pieces.append(spread(row_group, "row", col_index * groups + offset))
    item_panel = jnp.concatenate(pieces, axis=0)
    gram_matrix = lax.psum(
        jnp.dot(factor.T, factor, precision=lax.Precision.HIGHEST), ("row", "col")
    )
    tiles_now = masked_tiles(tile_values, tile_patterns)
    panel_tiles = item_panel.reshape(-1, tile_edge, rank_width)
    blocks = panel_tiles[tile_cols]
    products = jnp.einsum("sij,sjk->sik", tiles_now, blocks, precision=lax.Precision.HIGHEST)
    tile_row_count = col_count * items_here // tile_edge
    live_slots = jnp.arange(slot_count, dtype=jnp.int32) < tile_counts[0]
    selector = (
        tile_rows[None, :] == jnp.arange(tile_row_count, dtype=jnp.int32)[:, None]
    ) & live_slots[None, :]
    partial_rows = jnp.dot(
        selector.astype(jnp.float32),
        products.reshape(slot_count, tile_edge * rank_width),
        precision=lax.Precision.HIGHEST,
    )
    partial_rows = partial_rows.reshape(tile_row_count * tile_edge, rank_width)
    image = lax.psum_scatter(partial_rows, "col", scatter_dimension=0, tiled=True)
    return hals_sweep(factor, image, gram_matrix)


def solution(mesh):
    return jax.shard_map(
        shards,
        mesh=mesh,
        in_specs=(
            P(("row", "col"), None, None),
            P(("row", "col")),
            P(("row", "col")),
            P(("row", "col")),
            P(("row", "col")),
            P(("row", "col"), None),
        ),
        out_specs=P(("row", "col"), None),
        check_vma=False,
    )
```

profile of v0, /device:TPU:0, one launch (start us, length us, event | category | flops | bytes accessed | tf_op | source)
XLA Modules:
  0.0 478.0 jit_solution(6145449104703760734)
XLA Ops:
  6.5 1.9 copy.38
  8.5 35.4 %all-gather.2.cloned.1.call-done = f32[16384,64]{0,1:T(8,128)} async-done(((f32[2048,64]{0,1:T(8,128)}), f32[16384,64]{0,1:T(8,128)}) %all-gather.2.cloned.1.call-update) | async-done | bytes 4194320 | tf_op jit(solution)/shard_map/all_gather | solution.py:49
  43.9 6.2 %broadcast_select_fusion.1 = (f32[16384,64]{0,1:T(8,128)}, f32[16384,64]{0,1:T(8,128)}) fusion(f32[16384,64]{0,1:T(8,128)} %all-gather.2.cloned.1.call-done, pred[]{:T(512)S(6)} %eq.22, pred[]{:T(512)S(6)} %eq.23), kind=kLoop, calls=%fused_computation.12 | loop fusion | flops 2097152 | bytes 12582914 | tf_op jit(solution)/shard_map/jit(_where)/select_n | solution.py:9
  50.2 12.2 %mul.15 = f32[320,4,32,4,32]{0,4,3,2,1:T(8,128)} broadcast(f32[320,4,4]{0,2,1:T(4,128)S(1)} %and_convert_fusion), dimensions={0,1,3} | broadcast | bytes 20992000 | tf_op jit(solution)/shard_map/mul | solution.py:22
  62.4 23.9 %copy.20 = f32[320,128,128]{2,1,0:T(8,128)} copy(f32[320,128,128]{0,2,1:T(8,128)} %bitcast.33) | data formatting | bytes 41943040 | tf_op jit(solution)/shard_map/mul | solution.py:22
  87.0 104.6 %all-reduce.3.cloned.1.call-done = (f32[16384,64]{0,1:T(8,128)}, f32[16384,64]{0,1:T(8,128)}) async-done(((f32[16384,64]{0,1:T(8,128)}, f32[16384,64]{0,1:T(8,128)}), (f32[16384,64]{0,1:T(8,128)}, f32[16384,64]{0,1:T(8,128)})) %all-reduce.3.cloned.1.call-update) | async-done | bytes 8388624 | tf_op jit(solution)/shard_map/psum | solution.py:9
  191.7 6.2 %copy_bitcast_fusion = f32[256,128,64]{1,2,0:T(8,128)} fusion(f32[16384,64]{0,1:T(8,128)} %get-tuple-element.154, f32[16384,64]{0,1:T(8,128)} %get-tuple-element.155), kind=kLoop, calls=%fused_computation.9 | loop fusion | flops 2097152 | bytes 16777216 | tf_op jit(solution)/shard_map/reshape | solution.py:58
  197.9 8.6 %gather_fusion = f32[320,128,64]{1,2,0:T(8,128)} fusion(f32[256,128,64]{1,2,0:T(8,128)} %copy_bitcast_fusion, s32[1024]{0:T(1024)S(1)} %pad_clamp_fusion), kind=kCustom, calls=%fused_computation | custom fusion | bytes 20972800 | tf_op jit(solution)/shard_map/gather | solution.py:59
  206.4 46.3 %fusion.4 = f32[320,128,64]{1,2,0:T(8,128)} fusion(f32[320,128,64]{1,2,0:T(8,128)} %gather_fusion, f32[320,128,128]{2,1,0:T(8,128)} %param.8, f32[320,128,128]{2,1,0:T(8,128)} %copy.20), kind=kOutput, calls=%fused_computation.7 | convolution fusion | flops 4031774720 | bytes 62914560 | tf_op jit(solution)/shard_map/sij,sjk->sik/dot_general | solution.py:60
  252.8 12.0 %copy.22 = f32[320,128,64]{0,2,1:T(8,128)} copy(f32[320,128,64]{1,2,0:T(8,128)} %fusion.4) | data formatting | bytes 20971520 | tf_op jit(solution)/shard_map/sij,sjk->sik/dot_general | solution.py:60
  264.8 11.0 %fusion.7 = f32[128,8192]{1,0:T(8,128)} fusion(f32[320,8192]{0,1:T(8,128)} %bitcast.34, s32[320]{0:T(512)S(1)} %copy-done.4, pred[320]{0:T(512)(128)(4,1)S(1)} %iota_compare_fusion.1), kind=kOutput, calls=%fused_computation.15 | convolution fusion | flops 4026613760 | bytes 14681664 | tf_op jit(solution)/shard_map/dot_general | solution.py:66
  275.8 7.9 %reshape.59 = f32[16384,64]{1,0:T(8,128)} reshape(f32[128,8192]{1,0:T(8,128)} %fusion.7) | data formatting | bytes 8388608 | tf_op jit(solution)/shard_map/reshape | solution.py:71
  284.3 65.4 %psum.23 = f32[64,64]{1,0:T(8,128)S(1)} all-reduce(f32[64,64]{1,0:T(8,128)S(1)} %fusion.11), channel_id=1, replica_groups=mesh['row'=16,'col'=8] {'row','col'}, use_global_device_ids=true, to_apply=%region_0.1 | all-reduce | flops 4096 | bytes 32768 | tf_op jit(solution)/shard_map/psum | solution.py:54
  349.8 1.5 copy.23
  351.4 119.3 %while.16 = (s32[]{:T(128)}, f32[2048,64]{0,1:T(8,128)S(1)}, f32[2048,64]{0,1:T(8,128)S(1)}, f32[64,64]{0,1:T(8,128)S(1)}, s32[]{:T(128)}, /*index=5*/s32[]{:T(128)}, s32[]{:T(128)}) while((s32[]{:T(128)}, f32[2048,64]{0,1:T(8,128)S(1)}, f32[2048,64]{0,1:T(8,128)S(1)}, f32[64,64]{0,1:T(8,128)S(1)}, s32[]{:T(128)}, /*index=5*/s32[]{:T(128)}, ...), condition=%wide.region_5.6_spmd, body=%wide.region_4.5_spmd.sunk | while | flops 1581059 | bytes 567405 | solution.py:37
  352.0 1.0 fusion.20
  353.9 1.0 fusion.20
  355.8 1.0 fusion.20
  357.6 1.0 fusion.20
  359.5 1.0 fusion.20
  361.4 1.0 fusion.20
  363.2 1.0 fusion.20
  365.1 1.0 fusion.20
  366.9 1.0 fusion.20
  368.8 1.0 fusion.20
  370.7 1.0 fusion.20
  372.5 1.0 fusion.20
  374.4 1.0 fusion.20
  376.3 1.0 fusion.20
  378.1 1.0 fusion.20
  380.0 1.0 fusion.20
  381.9 1.0 fusion.20
  383.7 1.0 fusion.20
  385.6 1.0 fusion.20
  387.5 1.0 fusion.20
  389.3 1.0 fusion.20
  391.2 1.0 fusion.20
  393.1 1.0 fusion.20
  394.9 1.0 fusion.20
  396.8 1.0 fusion.20
  398.6 1.0 fusion.20
  400.5 1.0 fusion.20
  402.4 1.0 fusion.20
  404.2 1.0 fusion.20
  406.1 1.0 fusion.20
  408.0 1.0 fusion.20
  409.8 1.0 fusion.20
  411.7 1.0 fusion.20
  413.6 1.0 fusion.20
  415.4 1.0 fusion.20
  417.3 1.0 fusion.20
  419.1 1.0 fusion.20
  426.6 1.0 fusion.20
  428.5 1.0 fusion.20
  430.3 1.0 fusion.20
  432.2 1.0 fusion.20
  434.1 1.0 fusion.20
  435.9 1.0 fusion.20
  437.8 1.0 fusion.20
  439.7 1.0 fusion.20
  443.4 1.0 fusion.20
  447.1 1.0 fusion.20
  463.9 1.0 fusion.20
  467.6 1.0 fusion.20
  (167 shorter events, 70.5 us)
Async XLA Ops:
  6.5 37.3 %all-gather.2.cloned.1.call-start = ((), (), s32[]{:S(2)}) async-start(), calls=%async_computation.1 | async-start | bytes 4718592 | tf_op jit(solution)/shard_map/all_gather | solution.py:49
  8.4 183.2 %all-reduce.3.cloned.1.call-start = ((), (), s32[]{:S(2)}) async-start(), calls=%async_computation.3 | async-start | bytes 16777216 | tf_op jit(solution)/shard_map/psum | solution.py:9
  8.5 41.7 %copy-start.2 = (s32[320]{0:T(512)S(1)}, s32[320]{0:T(512)}, u32[]{:S(2)}) copy-start(s32[320]{0:T(512)} %param.11) | copy-start | bytes 3844
  50.1 299.7 %reduce-scatter.2.cloned.1.call-start = ((), (), s32[]{:S(2)}) async-start(), calls=%async_computation.2 | async-start | bytes 9437184 | tf_op jit(solution)/shard_map/reduce_scatter | solution.py:72
  62.4 24.6 %copy-start.3 = (s32[320]{0:T(512)S(1)}, s32[320]{0:T(512)}, u32[]{:S(2)}) copy-start(s32[320]{0:T(512)} %param.10) | copy-start | bytes 3844
  252.8 12.0 %copy-start.4 = (s32[320]{0:T(512)S(1)}, s32[320]{0:T(512)}, u32[]{:S(2)}) copy-start(s32[320]{0:T(512)} %param.9) | copy-start | bytes 3844
  275.8 8.0 %copy-start = (f32[2048,64]{0,1:T(8,128)S(1)}, f32[2048,64]{0,1:T(8,128)}, u32[]{:S(2)}) copy-start(f32[2048,64]{0,1:T(8,128)} %copy.38) | copy-start | bytes 1572868
  470.7 0.8 copy-start.1
Sparse Core Ops, SparseCore 0:
  9.0 34.7 all-gather.1
  50.2 141.3 all-reduce.2
  283.9 52.7 reduce-scatter.1
where the time goes:
time: 484 us; the launch traced here: 478 us
  waiting for transfers between devices  140 us (29%)
  local copies, waits for them, and re-layouts  123 us (25%)
  matrix products  121 us (25%)
  blocking collectives  65.4 us (14%)
  between operations  13.9 us (3%)
  other arithmetic  12.5 us (3%)
    psum x1, waiting for transfers between devices, spread(): return lax.psum(jnp.where(mine, shard, jnp.zeros_like(shard)), axis)  105 us
    psum x1, blocking collectives, shards(): lax.psum(jnp.dot(factor.T, factor, precision=lax.Precision.HIGHEST), ('ro...  65.4 us
    dot_general x64, matrix products, update(): fitted = jnp.dot(current, gram_col, precision=lax.Precision.HIGHEST)[:, 0]  63.4 us
    dot_general x1, matrix products, shards(): jnp.einsum('sij,sjk->sik', tiles_now, blocks, precision=lax.Precision.HIG...  46.3 us
    dynamic_slice x64, local copies, waits for them, and re-layouts, update(): diagonal = lax.dynamic_index_in_dim(gram_col[:, 0], column, 0, False)  40.9 us
    mul x2, local copies, waits for them, and re-layouts, masked_tiles(): values.reshape(count_tiles, 4, edge, 4, edge)  36.1 us
    all_gather x1, waiting for transfers between devices, shards(): row_group = lax.all_gather(factor, 'col', axis=0, tiled=True)  35.4 us
    dynamic_update_slice x64, local copies, waits for them, and re-layouts, update(): return lax.dynamic_update_index_in_dim(current, fresh, column, 1)  13.1 us
  transfers between devices with their start and end apart: 3, of which 2 were waited for; matrix products, arithmetic and copies ran while one was open for 8% of the time, Pallas kernels for 0%

commit v1 on v0

v1 whole, which is shorter than its diff:
```python
import functools

import jax
import jax.numpy as jnp
from jax import lax
from jax.experimental import pallas as pl
from jax.experimental.pallas import tpu as pltpu
from jax.sharding import PartitionSpec as P

NX = NY = NZ = 4
AXES = ("row", "col")
RANK, TILE, SLOTS = 64, 128, 320
PAIRS = 1
WIDTH = RANK // PAIRS
GRAM_ROWS = RANK * RANK // TILE
HALF = 8
ITEM_TILES = 16
ROW_TILES = 128
DUMMY = ROW_TILES
UNROLL = 8
BATCH = 32
PLACE = (0, 2, 3, 1)

WHOLE = pl.BlockSpec(memory_space=pltpu.VMEM)
SCALARS = pl.BlockSpec(memory_space=pltpu.SMEM)


def params(mib):
    return pltpu.CompilerParams(vmem_limit_bytes=mib * 2**20)


def coords(d):
    return d // 32, (d // 8) % 4, (d // 2) % 4, d % 2


def number(x, y, z, core):
    return ((x * NY + y) * NZ + z) * 2 + core


def shift(array, axis, step):
    pairs = []
    for d in range(128):
        place = list(coords(d))
        place[axis] = (place[axis] + step) % (2 if axis == 3 else 4)
        pairs.append((d, number(*place)))
    return lax.ppermute(array, AXES, pairs)


def spread(array):
    pairs = []
    for d in range(128):
        x, y, z, core = coords(d)
        pairs.append((d, number((x + z) % 4, y if core == 0 else 3 - y, x, y // 2)))
    return lax.ppermute(array, AXES, pairs)


def ring(block, axis):
    half = block.shape[0] // 2
    below, above = shift(block, axis, 1), shift(block, axis, -1)
    far = jnp.concatenate([shift(below[:half], axis, 1), shift(above[half:], axis, -1)])
    return [block, below, above, far]


def first_kernel(factor_ref, *outs):
    gram = jnp.zeros((RANK, RANK), jnp.float32)
    for tile in range(ITEM_TILES):
        piece = factor_ref[:, tile * TILE : (tile + 1) * TILE]
        gram += lax.dot_general(
            piece, piece, (((1,), (1,)), ((), ())), precision=lax.Precision.HIGHEST, preferred_element_type=jnp.float32
        )
        side, place = tile // HALF, tile % HALF
        for pair in range(PAIRS):
            outs[2 * pair + side][place * WIDTH : (place + 1) * WIDTH, :] = piece[pair * WIDTH : (pair + 1) * WIDTH]
    outs[0][HALF * WIDTH :, :] = jnp.concatenate([gram[:GRAM_ROWS], gram[GRAM_ROWS:]], axis=1)


def first(factor):
    rows = HALF * WIDTH
    shapes = []
    for pair in range(PAIRS):
        shapes += [rows + (GRAM_ROWS if pair == 0 else 0), rows]
    return pl.pallas_call(
        first_kernel,
        in_specs=[WHOLE],
        out_specs=[WHOLE] * (2 * PAIRS),
        out_shape=[jax.ShapeDtypeStruct((n, TILE), jnp.float32) for n in shapes],
        compiler_params=params(8),
        name="first",
    )(factor)


def split(value):
    high = value.astype(jnp.bfloat16)
    return high, (value - high.astype(jnp.float32)).astype(jnp.bfloat16)


def prepare_kernel(count, patterns, values_ref, tiles_ref):
    step = pl.program_id(0)
    bit = 4 * (lax.broadcasted_iota(jnp.int32, (TILE, TILE), 0) // 32)
    bit += lax.broadcasted_iota(jnp.int32, (TILE, TILE), 1) // 32
    flag = jnp.left_shift(1, bit)

    @pl.when(step * BATCH < count[0])
    def _():
        for u in range(BATCH):
            slot = step * BATCH + u
            kept = jnp.where((patterns[slot] & flag) != 0, values_ref[u], 0.0)
            high, low = split(kept.T)
            tiles_ref[slot, :TILE, :] = high
            tiles_ref[slot, TILE:, :] = low


def prepare(count, patterns, values):
    return pl.pallas_call(
        prepare_kernel,
        grid_spec=pltpu.PrefetchScalarGridSpec(
            num_scalar_prefetch=2,
            grid=(SLOTS // BATCH,),
            in_specs=[
                pl.BlockSpec(
                    (BATCH, TILE, TILE), lambda i, count, pats: (jnp.minimum(i, (count[0] - 1) // BATCH), 0, 0)
                )
            ],
            out_specs=WHOLE,
        ),
        out_shape=pltpu.VMEM((SLOTS, 2 * TILE, TILE), jnp.bfloat16),
        compiler_params=params(30),
        name="prepare",
    )(count, patterns, values)


def plan(rows, cols, count):
    row, col = lax.axis_index("row"), lax.axis_index("col")
    x, y, z, core = row // NY, row % NY, col // 2, col % 2
    shard, tile = cols // ITEM_TILES, cols % ITEM_TILES
    from_z, from_core = (shard % 8) // 2, shard % 2
    from_y = 2 * core + shard // 8
    to_x = (z + from_z) % NX
    to_y = jnp.where(from_core == 0, from_y, 3 - from_y)
    place = jnp.array(PLACE, jnp.int32)

    def placed(d):
        return jnp.where(d == 0, 0, jnp.where(d == 1, 2, jnp.where(d == 2, 3, 1)))

    px, py = placed((to_x - x) % 4), placed((to_y - y) % 4)
    side = tile // HALF
    part = jnp.where(side == 0, py, px)
    block = jnp.where(side == 0, px, py)
    owner = rows // ITEM_TILES
    target = ((owner % 2 + core) % 2) * 64 + ((owner // 2 - z) % 4) * ITEM_TILES + rows % ITEM_TILES
    slots = jnp.arange(SLOTS, dtype=jnp.int32)
    packed = slots + target * 512 + block * 131072 + (tile % HALF) * 524288
    key = jnp.where(slots < count[0], part * 2 + side, 8)
    before = (key[None, :] < key[:, None]) | ((key[None, :] == key[:, None]) & (slots[None, :] < slots[:, None]))
    position = jnp.sum(before.astype(jnp.int32), axis=1)
    places = jnp.arange(SLOTS + 2 * UNROLL, dtype=jnp.int32)
    order = jnp.sum(jnp.where(position[None, :] == places[:, None], packed[None, :], 0), axis=1)
    starts = jnp.sum((key[None, :] < jnp.arange(9, dtype=jnp.int32)[:, None]).astype(jnp.int32), axis=1)
    return order, starts


def products(order, lower, upper, tiles_ref, panel_ref, stride, sums_ref):
    def body(group, carry):
        found = []
        for u in range(UNROLL):
            at = lower + group * UNROLL + u
            word = order[at]
            slot = word & 511
            target = jnp.where(at < upper, (word >> 9) & 255, DUMMY)
            start = ((word >> 17) & 3) * stride + ((word >> 19) & 7) * WIDTH
            high, low = split(panel_ref[pl.ds(pl.multiple_of(start, 8), WIDTH), :])
            both = jnp.concatenate([high, low], axis=0)
            result = jnp.dot(
                jnp.concatenate([both, both], axis=1), tiles_ref[slot], preferred_element_type=jnp.float32
            )
            found.append((target, result[:WIDTH] + result[WIDTH:]))
        for target, result in found:
            sums_ref[pl.ds(pl.multiple_of(target * WIDTH, 8), WIDTH), :] += result
        return carry

    lax.fori_loop(0, (upper - lower + UNROLL - 1) // UNROLL, body, 0)


def part_kernel(part, with_gram, order, starts, tiles_ref, a_ref, b_ref, old_ref, sums_ref):
    stride = a_ref.shape[0] // 4
    bottom = (ROW_TILES + 1) * WIDTH
    if part == 0:
        sums_ref[...] = jnp.zeros_like(sums_ref)
    if with_gram:
        for block in range(4):
            sums_ref[bottom:, :] += a_ref[block * stride + HALF * WIDTH : (block + 1) * stride, :]
    products(order, starts[2 * part], starts[2 * part + 1], tiles_ref, a_ref, stride, sums_ref)
    products(order, starts[2 * part + 1], starts[2 * part + 2], tiles_ref, b_ref, HALF * WIDTH, sums_ref)


def add_part(part, with_gram, order, starts, tiles, a, b, sums):
    rows = (ROW_TILES + 1) * WIDTH + (GRAM_ROWS if with_gram else 0)
    kernel = functools.partial(part_kernel, part, with_gram)
    operands = [order, starts, tiles, a, b]
    if part > 0:
        operands.append(sums)
    else:
        kernel = functools.partial(lambda k, *refs: k(*refs[:5], None, refs[5]), kernel)
    return pl.pallas_call(
        kernel,
        in_specs=[SCALARS] * 2 + [WHOLE] * (len(operands) - 2),
        out_specs=WHOLE,
        out_shape=pltpu.VMEM((rows, TILE), jnp.float32),
        input_output_aliases={5: 0} if part > 0 else {},
        compiler_params=params(6),
        name="part",
    )(*operands)


def deal_kernel(with_gram, sums_ref, core_ref):
    rows = 64 * WIDTH
    core_ref[:rows, :] = sums_ref[rows : 2 * rows, :]
    if with_gram:
        core_ref[rows:, :] = sums_ref[2 * rows + WIDTH :, :]


def deal(with_gram, sums):
    rows = 64 * WIDTH + (GRAM_ROWS if with_gram else 0)
    return pl.pallas_call(
        functools.partial(deal_kernel, with_gram),
        in_specs=[WHOLE],
        out_specs=WHOLE,
        out_shape=jax.ShapeDtypeStruct((rows, TILE), jnp.float32),
        compiler_params=params(12),
        name="deal",
    )(sums)


def joined_kernel(with_gram, sums_ref, other_ref, up_ref, down_ref, kept_ref):
    block = ITEM_TILES * WIDTH
    half = block // 2
    total = 4 * block

    def both(start, size):
        return sums_ref[start : start + size, :] + other_ref[start : start + size, :]

    up_ref[:half, :] = both(2 * block, half)
    down_ref[:half, :] = both(2 * block + half, half)
    for place, source in enumerate((0, 1, 3)):
        kept_ref[place * block : (place + 1) * block, :] = both(source * block, block)
    if with_gram:
        gram = sums_ref[2 * total + WIDTH :, :] + other_ref[total:, :]
        up_ref[half:, :] = gram
        down_ref[half:, :] = gram
        kept_ref[3 * block :, :] = gram


def joined(with_gram, sums, other):
    block = ITEM_TILES * WIDTH
    extra = GRAM_ROWS if with_gram else 0
    shapes = [block // 2 + extra, block // 2 + extra, 3 * block + extra]
    return pl.pallas_call(
        functools.partial(joined_kernel, with_gram),
        in_specs=[WHOLE] * 2,
        out_specs=[WHOLE] * 3,
        out_shape=[jax.ShapeDtypeStruct((n, TILE), jnp.float32) for n in shapes],
        compiler_params=params(16),
        name="joined",
    )(sums, other)


def onward_kernel(with_gram, kept_ref, below_ref, above_ref, up_ref, down_ref):
    block = ITEM_TILES * WIDTH
    half = block // 2
    up_ref[:half, :] = kept_ref[block : block + half, :] + below_ref[:half, :]
    up_ref[half:block, :] = kept_ref[block + half : 2 * block, :]
    down_ref[:half, :] = kept_ref[2 * block : 2 * block + half, :]
    down_ref[half:block, :] = kept_ref[2 * block + half : 3 * block, :] + above_ref[:half, :]
    if with_gram:
        up_ref[block:, :] = below_ref[half:, :]


def onward(with_gram, kept, below, above):
    block = ITEM_TILES * WIDTH
    extra = GRAM_ROWS if with_gram else 0
    return pl.pallas_call(
        functools.partial(onward_kernel, with_gram),
        in_specs=[WHOLE] * 3,
        out_specs=[WHOLE] * 2,
        out_shape=[jax.ShapeDtypeStruct((n, TILE), jnp.float32) for n in (block + extra, block)],
        compiler_params=params(12),
        name="onward",
    )(kept, below, above)


def scatter(with_gram, sums):
    other = shift(deal(with_gram, sums), 3, 1)
    up, down, kept = joined(with_gram, sums, other)
    below, above = shift(up, 2, 1), shift(down, 2, -1)
    up, down = onward(with_gram, kept, below, above)
    return kept, below, above, shift(up, 2, 1), shift(down, 2, -1)


def sweep_kernel(*refs):
    blocks = refs[: 7 * PAIRS]
    out_ref, resid, state, moves, gram_ref, inverse_ref, gram_s, inverse_s, sems = refs[7 * PAIRS :]
    block = ITEM_TILES * WIDTH
    kept, below, above, last = blocks[0], blocks[1], blocks[2], blocks[3]
    packed = (kept[3 * block :, :] + below[block // 2 :, :]) + (above[block // 2 :, :] + last[block:, :])
    gram_ref[...] = packed
    inverse_ref[...] = 1.0 / packed
    copies = [
        pltpu.make_async_copy(gram_ref, gram_s, sems.at[0]),
        pltpu.make_async_copy(inverse_ref, inverse_s, sems.at[1]),
    ]
    for copy in copies:
        copy.start()
    gram = jnp.concatenate([packed[:, :RANK], packed[:, RANK:]], axis=0)
    for tile in range(ITEM_TILES):
        side, place = tile // HALF, tile % HALF
        images, olds = [], []
        for pair in range(PAIRS):
            kept, _, _, up, down, a, b = blocks[7 * pair : 7 * pair + 7]
            rows = slice(tile * WIDTH, (tile + 1) * WIDTH)
            images.append(kept[rows, :] + (up[rows, :] + down[rows, :]))
            olds.append((a, b)[side][place * WIDTH : (place + 1) * WIDTH, :])
        image, old = jnp.concatenate(images, axis=0), jnp.concatenate(olds, axis=0)
        fitted = jnp.dot(gram, old, precision=lax.Precision.HIGHEST, preferred_element_type=jnp.float32)
        resid[tile * RANK : (tile + 1) * RANK, :] = image - fitted
        state[tile * RANK : (tile + 1) * RANK, :] = old
    for copy in copies:
        copy.wait()

    def entry(ref, j, k):
        return ref[j % GRAM_ROWS, (j // GRAM_ROWS) * RANK + k]

    def column(ref, k):
        return ref[pl.ds(k, ITEM_TILES, stride=RANK), :]

    for group in range(RANK // 8):
        columns = range(group * 8, group * 8 + 8)
        left = tuple(column(resid, k) for k in columns)
        if group:

            def earlier(k, left):
                move = moves[k]
                return tuple(r - move * entry(gram_s, j, k) for r, j in zip(left, columns))

            left = lax.fori_loop(0, group * 8, earlier, left, unroll=4)
        left = list(left)
        for i, k in enumerate(columns):
            old = column(state, k)
            fresh = jnp.maximum(old + left[i] * entry(inverse_s, k, k), 0.0)
            move = fresh - old
            moves[k] = move
            state[pl.ds(k, ITEM_TILES, stride=RANK), :] = fresh
            for m in range(i + 1, 8):
                left[m] = left[m] - move * entry(gram_s, columns[m], k)
    for tile in range(ITEM_TILES):
        out_ref[:, tile * TILE : (tile + 1) * TILE] = state[tile * RANK : (tile + 1) * RANK, :]


def sweep(parts):
    items = ITEM_TILES * TILE
    return pl.pallas_call(
        sweep_kernel,
        in_specs=[WHOLE] * len(parts),
        out_specs=WHOLE,
        out_shape=jax.ShapeDtypeStruct((RANK, items), jnp.float32),
        scratch_shapes=[
            pltpu.VMEM((ITEM_TILES * RANK, TILE), jnp.float32),
            pltpu.VMEM((ITEM_TILES * RANK, TILE), jnp.float32),
            pltpu.VMEM((RANK, ITEM_TILES, TILE), jnp.float32),
            pltpu.VMEM((GRAM_ROWS, TILE), jnp.float32),
            pltpu.VMEM((GRAM_ROWS, TILE), jnp.float32),
            pltpu.SMEM((GRAM_ROWS, TILE), jnp.float32),
            pltpu.SMEM((GRAM_ROWS, TILE), jnp.float32),
            pltpu.SemaphoreType.DMA((2,)),
        ],
        compiler_params=params(16),
        name="sweep",
    )(*parts)


def shards(tile_values, tile_rows, tile_cols, tile_patterns, tile_counts, factor):
    own = first(factor.T)
    order, starts = plan(tile_rows, tile_cols, tile_counts)
    tiles = prepare(tile_counts, tile_patterns, tile_values)
    parts = []
    for pair in range(PAIRS):
        a, b = own[2 * pair], own[2 * pair + 1]
        a_first, b_first = spread(a), spread(b)
        if pair == 0:
            a_first, b_first, tiles, order, starts = lax.optimization_barrier((a_first, b_first, tiles, order, starts))
        a_line = jnp.concatenate(ring(a_first, 0))
        b_line = jnp.concatenate(ring(b_first, 1))
        a_plane, b_plane = ring(a_line, 1), ring(b_line, 0)
        sums = None
        for part in range(4):
            sums = add_part(part, pair == 0, order, starts, tiles, a_plane[part], b_plane[part], sums)
        parts += [*scatter(pair == 0, sums), a, b]
    return sweep(parts).T


def solution(mesh):
    spec = P(("row", "col"))
    return jax.shard_map(
        shards,
        mesh=mesh,
        in_specs=(P(("row", "col"), None, None), spec, spec, spec, spec, P(("row", "col"), None)),
        out_specs=P(("row", "col"), None),
        check_vma=False,
    )
```

time: 484 us -> 129 us (0.27)
  matrix products: 121 us -> 0 us
  local copies, waits for them, and re-layouts: 123 us -> 2.07 us
  waiting for transfers between devices: 140 us -> 48.3 us
  blocking collectives: 65.4 us -> 0 us
  starting transfers between devices: 0.09 us -> 46.3 us
  Pallas kernels: 0 us -> 27.6 us
  between operations: 13.9 us -> 1.16 us
  other arithmetic: 12.5 us -> 2.13 us
    dot_general x67 -> x0, matrix products: 121 us -> none  [the longest x64 63.4 us: update(): fitted = jnp.dot(current, gram_col, precision=lax.Precision.HIGHEST)[:, 0]]
    psum x1 -> x0, waiting for transfers between devices: 105 us -> none  [spread(): return lax.psum(jnp.where(mine, shard, jnp.zeros_like(shard)), axis)]
    psum x1 -> x0, blocking collectives: 65.4 us -> none  [shards(): lax.psum(jnp.dot(factor.T, factor, precision=lax.Precision.HIGHEST), ('ro...]
    ppermute x0 -> x23, waiting for transfers between devices: none -> 48.3 us  [the longest x21 48.3 us: shift(): return lax.ppermute(array, AXES, pairs)]
    ppermute x0 -> x23, starting transfers between devices: none -> 46.3 us  [the longest x21 44.9 us: shift(): return lax.ppermute(array, AXES, pairs)]
    dynamic_slice x64 -> x0, local copies, waits for them, and re-layouts: 40.9 us -> none  [update(): diagonal = lax.dynamic_index_in_dim(gram_col[:, 0], column, 0, False)]
    mul x2 -> x0, local copies, waits for them, and re-layouts: 36.1 us -> none  [masked_tiles(): values.reshape(count_tiles, 4, edge, 4, edge)]
    all_gather x1 -> x0, waiting for transfers between devices: 35.4 us -> none  [shards(): row_group = lax.all_gather(factor, 'col', axis=0, tiled=True)]
  transfers between devices with their start and end apart: 3 -> 23, of which waited for: 2 -> 10; matrix products, arithmetic and copies ran while one was open for 8% -> 2% of each run, Pallas kernels for 0% -> 14%
where the time goes in v1:
time: 129 us; the launch traced here: 128 us
  waiting for transfers between devices  48.3 us (37%)
  starting transfers between devices  46.3 us (36%)
  Pallas kernels  27.6 us (21%)
  other arithmetic  2.13 us (2%)
  local copies, waits for them, and re-layouts  2.07 us (2%)
    ppermute x21, waiting for transfers between devices, shift(): return lax.ppermute(array, AXES, pairs)  48.3 us
    ppermute x21, starting transfers between devices, shift(): return lax.ppermute(array, AXES, pairs)  44.9 us
    pallas_call x4, Pallas kernels, add_part(): pl.pallas_call(kernel, in_specs=[SCALARS] * 2 + [WHOLE] * (len(operands)...  11.2 us
    pallas_call x1, Pallas kernels, prepare(): pl.pallas_call(prepare_kernel, grid_spec=pltpu.PrefetchScalarGridSpec(num...  9.71 us
    pallas_call x1, Pallas kernels, sweep(): pl.pallas_call(sweep_kernel, in_specs=[WHOLE] * len(parts), out_specs=WHO...  5.26 us
  transfers between devices with their start and end apart: 23, of which 10 were waited for; matrix products, arithmetic and copies ran while one was open for 2% of the time, Pallas kernels for 14%

profile of v1, /device:TPU:0, one launch (start us, length us, event | category | flops | bytes accessed | tf_op | source)
XLA Modules:
  0.0 127.6 jit_solution(785740997296361788)
XLA Ops:
  0.0 1.0 copy-done
  1.0 1.0 first.1
  2.0 0.7 collective-permute-start
  2.7 0.7 collective-permute-start.1
  4.1 0.7 add_select_fusion.17
  4.8 0.7 fusion.19
  5.6 0.1 convert_reduce_fusion.1.refs_1_.starts
  5.7 0.7 copy-done.1
  6.4 9.7 %prepare.1.refs_2_.tiles_ref = bf16[320,256,128]{2,1,0:T(8,128)(2,1)S(1)} custom-call(s32[1]{0:T(128)} %copy.21.count, s32[320]{0:T(512)S(1)} %copy-done.1, f32[320,128,128]{2,1,0:T(8,128)} %values_ref.1), custom_call_target="tpu_custom_call" | custom-call | tf_op jit(solution)/shard_map/prepare/pallas_call | solution.py:114
  16.1 0.2 convert_reduce_fusion
  16.3 0.2 select_reduce_fusion.refs_0_.order
  16.5 0.0 collective-permute-done.1
  16.5 0.0 collective-permute-done
  16.5 5.0 %collective-permute-start.10 = (f32[512,128]{1,0:T(8,128)S(1)}, f32[512,128]{1,0:T(8,128)S(1)}, u32[]{:S(2)}, u32[]{:S(2)}) collective-permute-start(f32[512,128]{1,0:T(8,128)S(1)} %collective-permute-done.1), channel_id=1, source_target_pairs={{0,8},{1,9},{2,10},{3,11},{4,12},{5,13},{6,14},{7,15},{8,16},{9,17... | collective-permute-start | bytes 786440 | tf_op jit(solution)/shard_map/ppermute | solution.py:46
  21.5 3.0 %collective-permute-start.11 = (f32[512,128]{1,0:T(8,128)S(1)}, f32[512,128]{1,0:T(8,128)S(1)}, u32[]{:S(2)}, u32[]{:S(2)}) collective-permute-start(f32[512,128]{1,0:T(8,128)S(1)} %collective-permute-done.1), channel_id=1, source_target_pairs={{0,24},{1,25},{2,26},{3,27},{4,28},{5,29},{6,30},{7,31},{8,0},{9,1... | collective-permute-start | bytes 786440 | tf_op jit(solution)/shard_map/ppermute | solution.py:46
  24.5 4.4 %collective-permute-start.2 = (f32[544,128]{1,0:T(8,128)S(1)}, f32[544,128]{1,0:T(8,128)S(1)}, u32[]{:S(2)}, u32[]{:S(2)}) collective-permute-start(f32[544,128]{1,0:T(8,128)S(1)} %collective-permute-done), channel_id=1, source_target_pairs={{0,32},{1,33},{2,34},{3,35},{4,36},{5,37},{6,38},{7,39},{8,40},{9,... | collective-permute-start | bytes 835592 | tf_op jit(solution)/shard_map/ppermute | solution.py:46
  28.9 3.3 %collective-permute-start.3 = (f32[544,128]{1,0:T(8,128)S(1)}, f32[544,128]{1,0:T(8,128)S(1)}, u32[]{:S(2)}, u32[]{:S(2)}) collective-permute-start(f32[544,128]{1,0:T(8,128)S(1)} %collective-permute-done), channel_id=1, source_target_pairs={{0,96},{1,97},{2,98},{3,99},{4,100},{5,101},{6,102},{7,103},{8,104... | collective-permute-start | bytes 835592 | tf_op jit(solution)/shard_map/ppermute | solution.py:46
  32.3 0.0 collective-permute-done.10
  32.3 0.1 collective-permute-start.12
  32.4 0.0 collective-permute-done.11
  32.4 3.3 %collective-permute-start.13 = (f32[256,128]{1,0:T(8,128)S(1)}, f32[256,128]{1,0:T(8,128)S(1)}, u32[]{:S(2)}, u32[]{:S(2)}) collective-permute-start(f32[256,128]{1,0:T(8,128)S(1)} %slice.37), channel_id=1, source_target_pairs={{0,24},{1,25},{2,26},{3,27},{4,28},{5,29},{6,30},{7,31},{8,0},{9,1... | collective-permute-start | bytes 393224 | tf_op jit(solution)/shard_map/ppermute | solution.py:46
  35.8 1.0 collective-permute-done.2
  36.8 0.9 collective-permute-start.4
  37.6 0.5 collective-permute-done.3
  38.2 3.8 %collective-permute-start.5 = (f32[272,128]{1,0:T(8,128)S(1)}, f32[272,128]{1,0:T(8,128)S(1)}, u32[]{:S(2)}, u32[]{:S(2)}) collective-permute-start(f32[272,128]{1,0:T(8,128)S(1)} %slice.33), channel_id=1, source_target_pairs={{0,96},{1,97},{2,98},{3,99},{4,100},{5,101},{6,102},{7,103},{8,104... | collective-permute-start | bytes 417800 | tf_op jit(solution)/shard_map/ppermute | solution.py:46
  42.0 0.0 collective-permute-done.12
  42.0 0.0 collective-permute-done.13
  42.1 0.5 collective-permute-start.14
  42.5 2.8 %collective-permute-start.16 = (f32[2048,128]{1,0:T(8,128)S(1)}, f32[2048,128]{1,0:T(8,128)S(1)}, u32[]{:S(2)}, u32[]{:S(2)}) collective-permute-start(f32[2048,128]{1,0:T(8,128)S(1)} %constant_dynamic-update-slice_fusion.5.refs_4_), channel_id=1, source_target_pairs={{0,96},{1,97},{2,98},{3,99},{4,100},{5,101},{6,102},{7,103},{8,104... | collective-permute-start | bytes 3145736 | tf_op jit(solution)/shard_map/ppermute | solution.py:46
  45.4 0.0 collective-permute-done.4
  45.4 0.0 collective-permute-done.5
  45.4 0.1 collective-permute-start.6
  45.5 3.2 %collective-permute-start.8 = (f32[2176,128]{1,0:T(8,128)S(1)}, f32[2176,128]{1,0:T(8,128)S(1)}, u32[]{:S(2)}, u32[]{:S(2)}) collective-permute-start(f32[2176,128]{1,0:T(8,128)S(1)} %constant_dynamic-update-slice_fusion.refs_3_), channel_id=1, source_target_pairs={{0,24},{1,25},{2,26},{3,27},{4,28},{5,29},{6,30},{7,31},{8,0},{9,1... | collective-permute-start | bytes 3342344 | tf_op jit(solution)/shard_map/ppermute | solution.py:46
  48.7 18.4 %collective-permute-done.14.b_ref = f32[2048,128]{1,0:T(8,128)S(1)} collective-permute-done((f32[2048,128]{1,0:T(8,128)S(1)}, f32[2048,128]{1,0:T(8,128)S(1)}, u32[]{:S(2)}, u32[]{:S(2)}) %collective-permute-start.14) | collective-permute-done | bytes 1048608 | tf_op jit(solution)/shard_map/ppermute | solution.py:46
  67.1 0.1 collective-permute-start.15
  67.2 0.5 collective-permute-done.16.b_ref
  67.7 3.1 %collective-permute-start.17 = (f32[1024,128]{1,0:T(8,128)S(1)}, f32[1024,128]{1,0:T(8,128)S(1)}, u32[]{:S(2)}, u32[]{:S(2)}) collective-permute-start(f32[1024,128]{1,0:T(8,128)S(1)} %slice.39), channel_id=1, source_target_pairs={{0,96},{1,97},{2,98},{3,99},{4,100},{5,101},{6,102},{7,103},{8,104... | collective-permute-start | bytes 1572872 | tf_op jit(solution)/shard_map/ppermute | solution.py:46
  70.8 2.3 %collective-permute-done.6.a_ref = f32[2176,128]{1,0:T(8,128)S(1)} collective-permute-done((f32[2176,128]{1,0:T(8,128)S(1)}, f32[2176,128]{1,0:T(8,128)S(1)}, u32[]{:S(2)}, u32[]{:S(2)}) %collective-permute-start.6) | collective-permute-done | bytes 1114144 | tf_op jit(solution)/shard_map/ppermute | solution.py:46
  73.1 0.1 collective-permute-start.7
  73.2 0.0 collective-permute-done.8.a_ref
  73.2 3.3 %collective-permute-start.9 = (f32[1088,128]{1,0:T(8,128)S(1)}, f32[1088,128]{1,0:T(8,128)S(1)}, u32[]{:S(2)}, u32[]{:S(2)}) collective-permute-start(f32[1088,128]{1,0:T(8,128)S(1)} %slice.35), channel_id=1, source_target_pairs={{0,24},{1,25},{2,26},{3,27},{4,28},{5,29},{6,30},{7,31},{8,0},{9,1... | collective-permute-start | bytes 1671176 | tf_op jit(solution)/shard_map/ppermute | solution.py:46
  76.5 3.2 %part.4.old_ref = f32[8288,128]{1,0:T(8,128)S(1)} custom-call(s32[336]{0:T(512)S(1)} %select_reduce_fusion.refs_0_.order, s32[9]{0:T(128)S(1)} %convert_reduce_fusion.1.refs_1_.starts, bf16[320,256,128]{2,1,0:T(8,128)(2,1)S(1)} %prepare.1.refs_2_.tiles_ref, f32[2176,128]{1,0:T(8,128)S(1)} %constant_dynamic-update-slice_fusion.refs_3_, ...), custom_call_target="tpu_custom_call" | custom-call | tf_op jit(solution)/shard_map/part/pallas_call | solution.py:204
  79.7 2.6 %part.5.old_ref = f32[8288,128]{1,0:T(8,128)S(1)} custom-call(s32[336]{0:T(512)S(1)} %select_reduce_fusion.refs_0_.order, s32[9]{0:T(128)S(1)} %convert_reduce_fusion.1.refs_1_.starts, bf16[320,256,128]{2,1,0:T(8,128)(2,1)S(1)} %prepare.1.refs_2_.tiles_ref, f32[2176,128]{1,0:T(8,128)S(1)} %collective-permute-done.6.a_ref, ...), custom_call_target="tpu_custom_call", output_to_operand_aliasing={{}: (5, {})} | custom-call | tf_op jit(solution)/shard_map/part/pallas_call | solution.py:204
  82.4 2.7 %part.6.old_ref = f32[8288,128]{1,0:T(8,128)S(1)} custom-call(s32[336]{0:T(512)S(1)} %select_reduce_fusion.refs_0_.order, s32[9]{0:T(128)S(1)} %convert_reduce_fusion.1.refs_1_.starts, bf16[320,256,128]{2,1,0:T(8,128)(2,1)S(1)} %prepare.1.refs_2_.tiles_ref, f32[2176,128]{1,0:T(8,128)S(1)} %collective-permute-done.8.a_ref, ...), custom_call_target="tpu_custom_call", output_to_operand_aliasing={{}: (5, {})} | custom-call | tf_op jit(solution)/shard_map/part/pallas_call | solution.py:204
  85.0 0.0 collective-permute-done.15
  85.0 0.0 collective-permute-done.17
  85.1 0.1 pad_maximum_fusion.1.b_ref
  85.1 2.8 %collective-permute-done.7 = f32[1088,128]{1,0:T(8,128)S(1)} collective-permute-done((f32[1088,128]{1,0:T(8,128)S(1)}, f32[1088,128]{1,0:T(8,128)S(1)}, u32[]{:S(2)}, u32[]{:S(2)}) %collective-permute-start.7) | collective-permute-done | bytes 557088 | tf_op jit(solution)/shard_map/ppermute | solution.py:46
  88.0 0.1 pad_maximum_fusion.a_ref
  88.0 2.7 %part.7.sums_ref = f32[8288,128]{1,0:T(8,128)S(1)} custom-call(s32[336]{0:T(512)S(1)} %select_reduce_fusion.refs_0_.order, s32[9]{0:T(128)S(1)} %convert_reduce_fusion.1.refs_1_.starts, bf16[320,256,128]{2,1,0:T(8,128)(2,1)S(1)} %prepare.1.refs_2_.tiles_ref, f32[2176,128]{1,0:T(8,128)S(1)} %pad_maximum_fusion.a_ref, ...), custom_call_target="tpu_custom_call", output_to_operand_aliasing={{}: (5, {})} | custom-call | tf_op jit(solution)/shard_map/part/pallas_call | solution.py:204
  90.7 0.1 deal.1
  90.8 0.1 collective-permute-start.18
  90.9 4.2 %collective-permute-done.18.other_ref = f32[4128,128]{1,0:T(8,128)S(1)} collective-permute-done((f32[4128,128]{1,0:T(8,128)S(1)}, f32[4128,128]{1,0:T(8,128)S(1)}, u32[]{:S(2)}, u32[]{:S(2)}) %collective-permute-start.18) | collective-permute-done | bytes 2113568 | tf_op jit(solution)/shard_map/ppermute | solution.py:46
  95.1 0.3 joined.1
  95.4 0.6 collective-permute-start.19
  96.0 4.1 %collective-permute-start.20 = (f32[544,128]{1,0:T(8,128)S(1)}, f32[544,128]{1,0:T(8,128)S(1)}, u32[]{:S(2)}, u32[]{:S(2)}) collective-permute-start(f32[544,128]{1,0:T(8,128)S(1)} %get-tuple-element.26), channel_id=1, source_target_pairs={{0,6},{1,7},{2,0},{3,1},{4,2},{5,3},{6,4},{7,5},{8,14},{9,15},{10,... | collective-permute-start | bytes 835592 | tf_op jit(solution)/shard_map/ppermute | solution.py:46
  100.1 6.9 %collective-permute-done.19.below_ref.refs_1_ = f32[544,128]{1,0:T(8,128)S(1)} collective-permute-done((f32[544,128]{1,0:T(8,128)S(1)}, f32[544,128]{1,0:T(8,128)S(1)}, u32[]{:S(2)}, u32[]{:S(2)}) %collective-permute-start.19) | collective-permute-done | bytes 278560 | tf_op jit(solution)/shard_map/ppermute | solution.py:46
  107.0 0.0 collective-permute-done.20.above_ref.refs_2_
  107.0 0.1 onward.1
  107.1 1.2 collective-permute-start.21
  108.3 2.1 %collective-permute-start.22 = (f32[1024,128]{1,0:T(8,128)S(1)}, f32[1024,128]{1,0:T(8,128)S(1)}, u32[]{:S(2)}, u32[]{:S(2)}) collective-permute-start(f32[1024,128]{1,0:T(8,128)S(1)} %get-tuple-element.28), channel_id=1, source_target_pairs={{0,6},{1,7},{2,0},{3,1},{4,2},{5,3},{6,4},{7,5},{8,14},{9,15},{10,... | collective-permute-start | bytes 1572872 | tf_op jit(solution)/shard_map/ppermute | solution.py:46
  110.4 10.8 %collective-permute-done.22.refs_4_ = f32[1024,128]{1,0:T(8,128)S(1)} collective-permute-done((f32[1024,128]{1,0:T(8,128)S(1)}, f32[1024,128]{1,0:T(8,128)S(1)}, u32[]{:S(2)}, u32[]{:S(2)}) %collective-permute-start.22) | collective-permute-done | bytes 524320 | tf_op jit(solution)/shard_map/ppermute | solution.py:46
  121.2 1.0 collective-permute-done.21.refs_3_
  122.2 5.3 %sweep.1 = f32[64,2048]{1,0:T(8,128)} custom-call(f32[3104,128]{1,0:T(8,128)S(1)} %get-tuple-element.24.kept_ref.refs_0_, f32[544,128]{1,0:T(8,128)S(1)} %collective-permute-done.19.below_ref.refs_1_, f32[544,128]{1,0:T(8,128)S(1)} %collective-permute-done.20.above_ref.refs_2_, f32[1056,128]{1,0:T(8,128)S(1)} %collective-permute-done.21.refs_3_, ...), custom_call_target="tpu_custom_call" | custom-call | tf_op jit(solution)/shard_map/sweep/pallas_call | solution.py:360
  (21 shorter events, 0.4 us)
Async XLA Ops:
  0.0 1.0 copy-start
  2.0 14.5 %collective-permute-start = (f32[544,128]{1,0:T(8,128)S(1)}, f32[544,128]{1,0:T(8,128)S(1)}, u32[]{:S(2)}, u32[]{:S(2)}) collective-permute-start(f32[544,128]{1,0:T(8,128)S(1)} %get-tuple-element.17.refs_5_), channel_id=1, source_target_pairs={{0,0},{1,24},{2,32},{3,56},{4,64},{5,88},{6,96},{7,120},{8,8},{9,1... | collective-permute-start | bytes 835592 | tf_op jit(solution)/shard_map/ppermute | solution.py:54
  2.7 13.8 %collective-permute-start.1 = (f32[512,128]{1,0:T(8,128)S(1)}, f32[512,128]{1,0:T(8,128)S(1)}, u32[]{:S(2)}, u32[]{:S(2)}) collective-permute-start(f32[512,128]{1,0:T(8,128)S(1)} %get-tuple-element.18.refs_6_), channel_id=1, source_target_pairs={{0,0},{1,24},{2,32},{3,56},{4,64},{5,88},{6,96},{7,120},{8,8},{9,1... | collective-permute-start | bytes 786440 | tf_op jit(solution)/shard_map/ppermute | solution.py:54
  5.7 0.7 copy-start.1
  16.5 15.8 %collective-permute-start.10 = (f32[512,128]{1,0:T(8,128)S(1)}, f32[512,128]{1,0:T(8,128)S(1)}, u32[]{:S(2)}, u32[]{:S(2)}) collective-permute-start(f32[512,128]{1,0:T(8,128)S(1)} %collective-permute-done.1), channel_id=1, source_target_pairs={{0,8},{1,9},{2,10},{3,11},{4,12},{5,13},{6,14},{7,15},{8,16},{9,17... | collective-permute-start | bytes 786440 | tf_op jit(solution)/shard_map/ppermute | solution.py:46
  21.5 10.9 %collective-permute-start.11 = (f32[512,128]{1,0:T(8,128)S(1)}, f32[512,128]{1,0:T(8,128)S(1)}, u32[]{:S(2)}, u32[]{:S(2)}) collective-permute-start(f32[512,128]{1,0:T(8,128)S(1)} %collective-permute-done.1), channel_id=1, source_target_pairs={{0,24},{1,25},{2,26},{3,27},{4,28},{5,29},{6,30},{7,31},{8,0},{9,1... | collective-permute-start | bytes 786440 | tf_op jit(solution)/shard_map/ppermute | solution.py:46
  24.5 12.3 %collective-permute-start.2 = (f32[544,128]{1,0:T(8,128)S(1)}, f32[544,128]{1,0:T(8,128)S(1)}, u32[]{:S(2)}, u32[]{:S(2)}) collective-permute-start(f32[544,128]{1,0:T(8,128)S(1)} %collective-permute-done), channel_id=1, source_target_pairs={{0,32},{1,33},{2,34},{3,35},{4,36},{5,37},{6,38},{7,39},{8,40},{9,... | collective-permute-start | bytes 835592 | tf_op jit(solution)/shard_map/ppermute | solution.py:46
  28.9 9.3 %collective-permute-start.3 = (f32[544,128]{1,0:T(8,128)S(1)}, f32[544,128]{1,0:T(8,128)S(1)}, u32[]{:S(2)}, u32[]{:S(2)}) collective-permute-start(f32[544,128]{1,0:T(8,128)S(1)} %collective-permute-done), channel_id=1, source_target_pairs={{0,96},{1,97},{2,98},{3,99},{4,100},{5,101},{6,102},{7,103},{8,104... | collective-permute-start | bytes 835592 | tf_op jit(solution)/shard_map/ppermute | solution.py:46
  32.3 9.7 %collective-permute-start.12 = (f32[256,128]{1,0:T(8,128)S(1)}, f32[256,128]{1,0:T(8,128)S(1)}, u32[]{:S(2)}, u32[]{:S(2)}) collective-permute-start(f32[256,128]{1,0:T(8,128)S(1)} %slice.36), channel_id=1, source_target_pairs={{0,8},{1,9},{2,10},{3,11},{4,12},{5,13},{6,14},{7,15},{8,16},{9,17... | collective-permute-start | bytes 393224 | tf_op jit(solution)/shard_map/ppermute | solution.py:46
  32.4 9.6 %collective-permute-start.13 = (f32[256,128]{1,0:T(8,128)S(1)}, f32[256,128]{1,0:T(8,128)S(1)}, u32[]{:S(2)}, u32[]{:S(2)}) collective-permute-start(f32[256,128]{1,0:T(8,128)S(1)} %slice.37), channel_id=1, source_target_pairs={{0,24},{1,25},{2,26},{3,27},{4,28},{5,29},{6,30},{7,31},{8,0},{9,1... | collective-permute-start | bytes 393224 | tf_op jit(solution)/shard_map/ppermute | solution.py:46
  36.8 8.6 %collective-permute-start.4 = (f32[272,128]{1,0:T(8,128)S(1)}, f32[272,128]{1,0:T(8,128)S(1)}, u32[]{:S(2)}, u32[]{:S(2)}) collective-permute-start(f32[272,128]{1,0:T(8,128)S(1)} %slice.32), channel_id=1, source_target_pairs={{0,32},{1,33},{2,34},{3,35},{4,36},{5,37},{6,38},{7,39},{8,40},{9,... | collective-permute-start | bytes 417800 | tf_op jit(solution)/shard_map/ppermute | solution.py:46
  38.2 7.2 %collective-permute-start.5 = (f32[272,128]{1,0:T(8,128)S(1)}, f32[272,128]{1,0:T(8,128)S(1)}, u32[]{:S(2)}, u32[]{:S(2)}) collective-permute-start(f32[272,128]{1,0:T(8,128)S(1)} %slice.33), channel_id=1, source_target_pairs={{0,96},{1,97},{2,98},{3,99},{4,100},{5,101},{6,102},{7,103},{8,104... | collective-permute-start | bytes 417800 | tf_op jit(solution)/shard_map/ppermute | solution.py:46
  42.1 25.0 %collective-permute-start.14 = (f32[2048,128]{1,0:T(8,128)S(1)}, f32[2048,128]{1,0:T(8,128)S(1)}, u32[]{:S(2)}, u32[]{:S(2)}) collective-permute-start(f32[2048,128]{1,0:T(8,128)S(1)} %constant_dynamic-update-slice_fusion.5.refs_4_), channel_id=1, source_target_pairs={{0,32},{1,33},{2,34},{3,35},{4,36},{5,37},{6,38},{7,39},{8,40},{9,... | collective-permute-start | bytes 3145736 | tf_op jit(solution)/shard_map/ppermute | solution.py:46
  42.5 25.2 %collective-permute-start.16 = (f32[2048,128]{1,0:T(8,128)S(1)}, f32[2048,128]{1,0:T(8,128)S(1)}, u32[]{:S(2)}, u32[]{:S(2)}) collective-permute-start(f32[2048,128]{1,0:T(8,128)S(1)} %constant_dynamic-update-slice_fusion.5.refs_4_), channel_id=1, source_target_pairs={{0,96},{1,97},{2,98},{3,99},{4,100},{5,101},{6,102},{7,103},{8,104... | collective-permute-start | bytes 3145736 | tf_op jit(solution)/shard_map/ppermute | solution.py:46
  45.4 27.7 %collective-permute-start.6 = (f32[2176,128]{1,0:T(8,128)S(1)}, f32[2176,128]{1,0:T(8,128)S(1)}, u32[]{:S(2)}, u32[]{:S(2)}) collective-permute-start(f32[2176,128]{1,0:T(8,128)S(1)} %constant_dynamic-update-slice_fusion.refs_3_), channel_id=1, source_target_pairs={{0,8},{1,9},{2,10},{3,11},{4,12},{5,13},{6,14},{7,15},{8,16},{9,17... | collective-permute-start | bytes 3342344 | tf_op jit(solution)/shard_map/ppermute | solution.py:46
  45.5 27.7 %collective-permute-start.8 = (f32[2176,128]{1,0:T(8,128)S(1)}, f32[2176,128]{1,0:T(8,128)S(1)}, u32[]{:S(2)}, u32[]{:S(2)}) collective-permute-start(f32[2176,128]{1,0:T(8,128)S(1)} %constant_dynamic-update-slice_fusion.refs_3_), channel_id=1, source_target_pairs={{0,24},{1,25},{2,26},{3,27},{4,28},{5,29},{6,30},{7,31},{8,0},{9,1... | collective-permute-start | bytes 3342344 | tf_op jit(solution)/shard_map/ppermute | solution.py:46
  67.1 17.9 %collective-permute-start.15 = (f32[1024,128]{1,0:T(8,128)S(1)}, f32[1024,128]{1,0:T(8,128)S(1)}, u32[]{:S(2)}, u32[]{:S(2)}) collective-permute-start(f32[1024,128]{1,0:T(8,128)S(1)} %slice.38), channel_id=1, source_target_pairs={{0,32},{1,33},{2,34},{3,35},{4,36},{5,37},{6,38},{7,39},{8,40},{9,... | collective-permute-start | bytes 1572872 | tf_op jit(solution)/shard_map/ppermute | solution.py:46
  67.7 17.3 %collective-permute-start.17 = (f32[1024,128]{1,0:T(8,128)S(1)}, f32[1024,128]{1,0:T(8,128)S(1)}, u32[]{:S(2)}, u32[]{:S(2)}) collective-permute-start(f32[1024,128]{1,0:T(8,128)S(1)} %slice.39), channel_id=1, source_target_pairs={{0,96},{1,97},{2,98},{3,99},{4,100},{5,101},{6,102},{7,103},{8,104... | collective-permute-start | bytes 1572872 | tf_op jit(solution)/shard_map/ppermute | solution.py:46
  73.1 14.9 %collective-permute-start.7 = (f32[1088,128]{1,0:T(8,128)S(1)}, f32[1088,128]{1,0:T(8,128)S(1)}, u32[]{:S(2)}, u32[]{:S(2)}) collective-permute-start(f32[1088,128]{1,0:T(8,128)S(1)} %slice.34), channel_id=1, source_target_pairs={{0,8},{1,9},{2,10},{3,11},{4,12},{5,13},{6,14},{7,15},{8,16},{9,17... | collective-permute-start | bytes 1671176 | tf_op jit(solution)/shard_map/ppermute | solution.py:46
  73.2 14.7 %collective-permute-start.9 = (f32[1088,128]{1,0:T(8,128)S(1)}, f32[1088,128]{1,0:T(8,128)S(1)}, u32[]{:S(2)}, u32[]{:S(2)}) collective-permute-start(f32[1088,128]{1,0:T(8,128)S(1)} %slice.35), channel_id=1, source_target_pairs={{0,24},{1,25},{2,26},{3,27},{4,28},{5,29},{6,30},{7,31},{8,0},{9,1... | collective-permute-start | bytes 1671176 | tf_op jit(solution)/shard_map/ppermute | solution.py:46
  90.8 4.3 %collective-permute-start.18 = (f32[4128,128]{1,0:T(8,128)S(1)}, f32[4128,128]{1,0:T(8,128)S(1)}, u32[]{:S(2)}, u32[]{:S(2)}) collective-permute-start(f32[4128,128]{1,0:T(8,128)S(1)} %deal.1), channel_id=1, source_target_pairs={{0,1},{1,0},{2,3},{3,2},{4,5},{5,4},{6,7},{7,6},{8,9},{9,8},{10,11... | collective-permute-start | bytes 6340616 | tf_op jit(solution)/shard_map/ppermute | solution.py:46
  95.4 11.6 %collective-permute-start.19 = (f32[544,128]{1,0:T(8,128)S(1)}, f32[544,128]{1,0:T(8,128)S(1)}, u32[]{:S(2)}, u32[]{:S(2)}) collective-permute-start(f32[544,128]{1,0:T(8,128)S(1)} %get-tuple-element.25), channel_id=1, source_target_pairs={{0,2},{1,3},{2,4},{3,5},{4,6},{5,7},{6,0},{7,1},{8,10},{9,11},{10,... | collective-permute-start | bytes 835592 | tf_op jit(solution)/shard_map/ppermute | solution.py:46
  96.0 11.0 %collective-permute-start.20 = (f32[544,128]{1,0:T(8,128)S(1)}, f32[544,128]{1,0:T(8,128)S(1)}, u32[]{:S(2)}, u32[]{:S(2)}) collective-permute-start(f32[544,128]{1,0:T(8,128)S(1)} %get-tuple-element.26), channel_id=1, source_target_pairs={{0,6},{1,7},{2,0},{3,1},{4,2},{5,3},{6,4},{7,5},{8,14},{9,15},{10,... | collective-permute-start | bytes 835592 | tf_op jit(solution)/shard_map/ppermute | solution.py:46
  107.1 15.1 %collective-permute-start.21 = (f32[1056,128]{1,0:T(8,128)S(1)}, f32[1056,128]{1,0:T(8,128)S(1)}, u32[]{:S(2)}, u32[]{:S(2)}) collective-permute-start(f32[1056,128]{1,0:T(8,128)S(1)} %get-tuple-element.27), channel_id=1, source_target_pairs={{0,2},{1,3},{2,4},{3,5},{4,6},{5,7},{6,0},{7,1},{8,10},{9,11},{10,... | collective-permute-start | bytes 1622024 | tf_op jit(solution)/shard_map/ppermute | solution.py:46
  108.3 12.9 %collective-permute-start.22 = (f32[1024,128]{1,0:T(8,128)S(1)}, f32[1024,128]{1,0:T(8,128)S(1)}, u32[]{:S(2)}, u32[]{:S(2)}) collective-permute-start(f32[1024,128]{1,0:T(8,128)S(1)} %get-tuple-element.28), channel_id=1, source_target_pairs={{0,6},{1,7},{2,0},{3,1},{4,2},{5,3},{6,4},{7,5},{8,14},{9,15},{10,... | collective-permute-start | bytes 1572872 | tf_op jit(solution)/shard_map/ppermute | solution.py:46

commit v2 on v1

v2 whole, which is shorter than its diff:
```python
import functools

import jax
import jax.numpy as jnp
from jax import lax
from jax.experimental import pallas as pl
from jax.experimental.pallas import tpu as pltpu
from jax.sharding import PartitionSpec as P

AXES = ("row", "col")
RANK, TILE, SLOTS = 64, 128, 320
HALF_RANK = RANK // 2
GRAM_ROWS = RANK * RANK // TILE
HALF = 8
ITEM_TILES = 16
ROW_TILES = 128
DUMMY = ROW_TILES
UNROLL = 8
BATCH = 32
A_ROWS = (HALF * RANK // 2 + GRAM_ROWS, HALF * RANK // 2)
B_ROWS = (HALF * RANK // 2, HALF * RANK // 2)
CHEAP = pl.CostEstimate(flops=1, bytes_accessed=1, transcendentals=0)

WHOLE = pl.BlockSpec(memory_space=pltpu.VMEM)
SCALARS = pl.BlockSpec(memory_space=pltpu.SMEM)


def params(mib):
    return pltpu.CompilerParams(vmem_limit_bytes=mib * 2**20)


def coords(d):
    return d // 32, (d // 8) % 4, (d // 2) % 4, d % 2


def number(x, y, z, core):
    return ((x * 4 + y) * 4 + z) * 2 + core


def permute(array, move):
    return lax.ppermute(array, AXES, [(d, number(*move(*coords(d)))) for d in range(128)])


def shift(array, axis, step):
    def move(*place):
        return [(p + step) % 4 if i == axis else p for i, p in enumerate(place)]

    return permute(array, move)


def swap_cores(array):
    return permute(array, lambda x, y, z, core: (x, y, z, 1 - core))


def swap(array, axis, across):
    def move(*place):
        return [(3 - p if across else p ^ 1) if i == axis else p for i, p in enumerate(place)]

    return permute(array, move)


def spread(array):
    return permute(array, lambda x, y, z, core: ((x + z + 2 * core) % 4, y if core == 0 else 3 - y, x, y // 2))


def line(head, tail, axis):
    heads = [head, swap(head, axis, False)]
    tails = [tail, swap(tail, axis, True)]
    return [*heads, swap(jnp.concatenate(heads), axis, True), *tails, swap(jnp.concatenate(tails), axis, False)]


def laid_kernel(*refs):
    pieces, out = refs[:-1], refs[-1]
    start = 0
    for piece in pieces:
        out[start : start + piece.shape[0], :] = piece[...]
        start += piece.shape[0]


def laid(pieces, rows):
    return pl.pallas_call(
        laid_kernel,
        in_specs=[WHOLE] * len(pieces),
        out_specs=WHOLE,
        out_shape=jax.ShapeDtypeStruct((4 * sum(rows), TILE), jnp.float32),
        cost_estimate=CHEAP,
        compiler_params=params(6),
        name="laid",
    )(*pieces)


def arranged_kernel(items_ref, *outs):
    for tile in range(HALF // 2, ITEM_TILES):
        start = tile % (HALF // 2) * RANK
        outs[tile // (HALF // 2) - 1][start : start + RANK, :] = items_ref[:, tile * TILE : (tile + 1) * TILE]


def head_kernel(items_ref, out):
    gram = jnp.zeros((RANK, RANK), jnp.float32)
    for tile in range(ITEM_TILES):
        piece = items_ref[:, tile * TILE : (tile + 1) * TILE]
        gram += lax.dot_general(
            piece, piece, (((1,), (1,)), ((), ())), precision=lax.Precision.HIGHEST, preferred_element_type=jnp.float32
        )
        if tile < HALF // 2:
            out[tile * RANK : (tile + 1) * RANK, :] = piece
    out[B_ROWS[0] :, :] = jnp.concatenate([gram[:GRAM_ROWS], gram[GRAM_ROWS:]], axis=1)


def arranged(items):
    def call(kernel, rows, name):
        return pl.pallas_call(
            kernel,
            in_specs=[WHOLE],
            out_specs=[WHOLE] * len(rows),
            out_shape=[jax.ShapeDtypeStruct((n, TILE), jnp.float32) for n in rows],
            cost_estimate=CHEAP,
            compiler_params=params(8),
            name=name,
        )(items)

    return *call(head_kernel, A_ROWS[:1], "head"), *call(arranged_kernel, A_ROWS[1:] + B_ROWS, "arranged")


def split(value):
    high = value.astype(jnp.bfloat16)
    return high, (value - high.astype(jnp.float32)).astype(jnp.bfloat16)


def prepare_kernel(count, patterns, values_ref, tiles_ref):
    step = pl.program_id(0)
    bit = 4 * (lax.broadcasted_iota(jnp.int32, (TILE, TILE), 0) // 32)
    bit += lax.broadcasted_iota(jnp.int32, (TILE, TILE), 1) // 32
    flag = jnp.left_shift(1, bit)

    @pl.when(step * BATCH < count[0])
    def _():
        for u in range(BATCH):
            slot = step * BATCH + u
            kept = jnp.where((patterns[slot] & flag) != 0, values_ref[u], 0.0)
            high, low = split(kept.T)
            tiles_ref[slot, :TILE, :] = high
            tiles_ref[slot, TILE:, :] = low


def prepare(count, patterns, values):
    def block(i, count, patterns):
        return jnp.minimum(i, (count[0] - 1) // BATCH), 0, 0

    return pl.pallas_call(
        prepare_kernel,
        grid_spec=pltpu.PrefetchScalarGridSpec(
            num_scalar_prefetch=2,
            grid=(SLOTS // BATCH,),
            in_specs=[pl.BlockSpec((BATCH, TILE, TILE), block)],
            out_specs=WHOLE,
        ),
        out_shape=pltpu.VMEM((SLOTS, 2 * TILE, TILE), jnp.bfloat16),
        cost_estimate=CHEAP,
        compiler_params=params(10),
        name="prepare",
    )(count, patterns, values)


def plan(rows, cols, count):
    row, col = lax.axis_index("row"), lax.axis_index("col")
    x, y, z, core = row // 4, row % 4, col // 2, col % 2
    shard, tile = cols // ITEM_TILES, cols % ITEM_TILES
    from_z, from_core = (shard % 8) // 2, shard % 2
    from_y = 2 * core + shard // 8
    to_x = (z + from_z + 2 * from_core) % 4
    to_y = jnp.where(from_core == 0, from_y, 3 - from_y)
    def ringed(to, here):
        d = (to - here) % 4
        return jnp.where(d == 0, 0, jnp.where(d == 3, 1, jnp.where(d == 1, 2, 3)))

    def swapped(to, here, second):
        near = to == (here ^ 1)
        across = to == 3 - here
        return jnp.where(to == here, 0, jnp.where(near, 1 + second, jnp.where(across, 2 - second, 3)))

    side, place = tile // HALF, tile % HALF
    second = place // (HALF // 2)
    part = jnp.where(side == 0, ringed(to_y, y), ringed(to_x, x))
    block = jnp.where(side == 0, swapped(to_x, x, second), swapped(to_y, y, second))
    head = jnp.where(side == 0, A_ROWS[0], B_ROWS[0])
    start = jnp.where(second == 0, block * head, 4 * head + block * B_ROWS[1]) + place % (HALF // 2) * RANK
    owner = rows // ITEM_TILES
    target = ((owner % 2 + core) % 2) * 64 + ((owner // 2 - z) % 4) * ITEM_TILES + rows % ITEM_TILES
    slots = jnp.arange(SLOTS, dtype=jnp.int32)
    packed = slots + target * 512 + start // 8 * 131072
    key = part * 2 + side + jnp.where((part == 3) & (target < 64), 2, 0)
    key = jnp.where(slots < count[0], key, 10)
    before = (key[None, :] < key[:, None]) | ((key[None, :] == key[:, None]) & (slots[None, :] < slots[:, None]))
    position = jnp.sum(before.astype(jnp.int32), axis=1)
    places = jnp.arange(SLOTS + 2 * UNROLL, dtype=jnp.int32)
    order = jnp.sum(jnp.where(position[None, :] == places[:, None], packed[None, :], 0), axis=1)
    starts = jnp.sum((key[None, :] < jnp.arange(11, dtype=jnp.int32)[:, None]).astype(jnp.int32), axis=1)
    return order, starts


def products(order, lower, upper, tiles_ref, panel_ref, sums_ref):
    def body(group, carry):
        found = []
        for u in range(UNROLL):
            at = lower + group * UNROLL + u
            word = jnp.where(at < upper, order[at], DUMMY * 512)
            target = (word >> 9) & 255
            high, low = split(panel_ref[pl.ds(pl.multiple_of((word >> 17) * 8, 8), RANK), :])
            both = jnp.concatenate([high, low], axis=0)
            result = jnp.dot(
                jnp.concatenate([both, both], axis=1), tiles_ref[word & 511], preferred_element_type=jnp.float32
            )
            found.append((target, result[:RANK] + result[RANK:]))
        for target, result in found:
            sums_ref[pl.ds(pl.multiple_of(target * RANK, 8), RANK), :] += result
        return carry

    lax.fori_loop(0, (upper - lower + UNROLL - 1) // UNROLL, body, 0)


def part_kernel(keys, fresh, order, starts, tiles_ref, *refs):
    panels, sums_ref = refs[: len(keys)], refs[-1]
    bottom = (ROW_TILES + 1) * RANK
    if fresh:
        sums_ref[...] = jnp.zeros_like(sums_ref)
    for key, panel_ref in zip(keys, panels):
        if key % 2 == 0 and key < 8:
            for block in range(4):
                gram = block * A_ROWS[0] + B_ROWS[0]
                sums_ref[bottom:, :] += panel_ref[gram : gram + GRAM_ROWS, :]
        products(order, starts[key], starts[key + 1], tiles_ref, panel_ref, sums_ref)


def add_parts(order, starts, tiles, parts, sums):
    keys = tuple(sorted(parts))
    operands = [order, starts, tiles] + [parts[key] for key in keys]
    if sums is not None:
        operands.append(sums)
    last = len(operands) - 1
    return pl.pallas_call(
        functools.partial(part_kernel, keys, sums is None),
        in_specs=[SCALARS] * 2 + [WHOLE] * (len(operands) - 2),
        out_specs=WHOLE,
        out_shape=pltpu.VMEM(((ROW_TILES + 1) * RANK + GRAM_ROWS, TILE), jnp.float32),
        input_output_aliases={} if sums is None else {last: 0},
        cost_estimate=CHEAP,
        compiler_params=params(6),
        name="part",
    )(*operands)


def half_of(ref, tile, half):
    return ref[tile * RANK + half * HALF_RANK : tile * RANK + (half + 1) * HALF_RANK, :]


def deal_kernel(sums_ref, *core_refs):
    for half, out in enumerate(core_refs):
        for tile in range(64):
            out[tile * HALF_RANK : (tile + 1) * HALF_RANK, :] = half_of(sums_ref, 64 + tile, half)
    core_refs[0][64 * HALF_RANK :, :] = sums_ref[(ROW_TILES + 1) * RANK :, :]


def deal(sums):
    rows = 64 * HALF_RANK
    return pl.pallas_call(
        deal_kernel,
        in_specs=[WHOLE],
        out_specs=[WHOLE] * 2,
        out_shape=[jax.ShapeDtypeStruct((n, TILE), jnp.float32) for n in (rows + GRAM_ROWS, rows)],
        cost_estimate=CHEAP,
        compiler_params=params(12),
        name="deal",
    )(sums)


def joined_kernel(half, sums_ref, other_ref, *outs):
    size = ITEM_TILES * HALF_RANK
    for place, out in enumerate(outs):
        for tile in range(ITEM_TILES):
            at = place * ITEM_TILES + tile
            rows = slice(tile * HALF_RANK, (tile + 1) * HALF_RANK)
            out[rows, :] = half_of(sums_ref, at, half) + other_ref[at * HALF_RANK : (at + 1) * HALF_RANK, :]
        if half == 0:
            out[size:, :] = sums_ref[(ROW_TILES + 1) * RANK :, :] + other_ref[4 * size :, :]


def joined(half, sums, other):
    rows = ITEM_TILES * HALF_RANK + (GRAM_ROWS if half == 0 else 0)
    return pl.pallas_call(
        functools.partial(joined_kernel, half),
        in_specs=[WHOLE] * 2,
        out_specs=[WHOLE] * 4,
        out_shape=[jax.ShapeDtypeStruct((rows, TILE), jnp.float32)] * 4,
        cost_estimate=CHEAP,
        compiler_params=params(12),
        name="joined",
    )(sums, other)


def onward_kernel(block_ref, passed_ref, out_ref):
    size = ITEM_TILES * HALF_RANK
    out_ref[:size, :] = block_ref[:size, :] + passed_ref[:size, :]
    if out_ref.shape[0] > size:
        out_ref[size:, :] = passed_ref[size:, :]


def onward(block, passed):
    return pl.pallas_call(
        onward_kernel,
        in_specs=[WHOLE] * 2,
        out_specs=WHOLE,
        out_shape=jax.ShapeDtypeStruct(block.shape, jnp.float32),
        cost_estimate=CHEAP,
        compiler_params=params(6),
        name="onward",
    )(block, passed)


def sweep_kernel(*refs):
    factor_ref, blocks = refs[0], refs[1:8]
    out_ref, resid, state, moves, gram_ref, inverse_ref, gram_s, inverse_s, sems = refs[8:]
    size = ITEM_TILES * HALF_RANK
    grams = [ref[size:, :] for ref in blocks[:4]]
    packed = (grams[0] + grams[1]) + (grams[2] + grams[3])
    gram_ref[...] = packed
    inverse_ref[...] = 1.0 / packed
    copies = [
        pltpu.make_async_copy(gram_ref, gram_s, sems.at[0]),
        pltpu.make_async_copy(inverse_ref, inverse_s, sems.at[1]),
    ]
    for copy in copies:
        copy.start()
    gram = jnp.concatenate([packed[:, :RANK], packed[:, RANK:]], axis=0)
    for tile in range(ITEM_TILES):
        rows = slice(tile * HALF_RANK, (tile + 1) * HALF_RANK)
        pieces = [ref[rows, :] for ref in blocks]
        image = jnp.concatenate(
            [pieces[0] + (pieces[2] + pieces[3]), pieces[4] + (pieces[5] + pieces[6])], axis=0
        )
        old = factor_ref[:, tile * TILE : (tile + 1) * TILE]
        fitted = jnp.dot(gram, old, precision=lax.Precision.HIGHEST, preferred_element_type=jnp.float32)
        resid[tile * RANK : (tile + 1) * RANK, :] = image - fitted
        state[tile * RANK : (tile + 1) * RANK, :] = old
    for copy in copies:
        copy.wait()

    def entry(ref, j, k):
        return ref[j % GRAM_ROWS, (j // GRAM_ROWS) * RANK + k]

    def column(ref, k):
        return ref[pl.ds(k, ITEM_TILES, stride=RANK), :]

    for group in range(RANK // 8):
        columns = range(group * 8, group * 8 + 8)
        if group == HALF_RANK // 8:
            for tile in range(ITEM_TILES):
                top, middle, bottom = tile * RANK, tile * RANK + HALF_RANK, (tile + 1) * RANK
                resid[middle:bottom, :] -= jnp.dot(
                    gram[HALF_RANK:, :HALF_RANK],
                    resid[top:middle, :],
                    precision=lax.Precision.HIGHEST,
                    preferred_element_type=jnp.float32,
                )
        left = tuple(column(resid, k) for k in columns)
        for k in range(group * 8 // HALF_RANK * HALF_RANK, group * 8):
            move = moves[k]
            left = tuple(r - move * entry(gram_s, j, k) for r, j in zip(left, columns))
        left = list(left)
        for i, k in enumerate(columns):
            old = column(state, k)
            fresh = jnp.maximum(old + left[i] * entry(inverse_s, k, k), 0.0)
            move = fresh - old
            moves[k] = move
            if k < HALF_RANK:
                resid[pl.ds(k, ITEM_TILES, stride=RANK), :] = move
            state[pl.ds(k, ITEM_TILES, stride=RANK), :] = fresh
            for m in range(i + 1, 8):
                left[m] = left[m] - move * entry(gram_s, columns[m], k)
    for tile in range(ITEM_TILES):
        out_ref[:, tile * TILE : (tile + 1) * TILE] = state[tile * RANK : (tile + 1) * RANK, :]


def sweep(parts):
    items = ITEM_TILES * TILE
    return pl.pallas_call(
        sweep_kernel,
        in_specs=[WHOLE] * len(parts),
        out_specs=WHOLE,
        out_shape=jax.ShapeDtypeStruct((RANK, items), jnp.float32),
        scratch_shapes=[
            pltpu.VMEM((ITEM_TILES * RANK, TILE), jnp.float32),
            pltpu.VMEM((ITEM_TILES * RANK, TILE), jnp.float32),
            pltpu.VMEM((RANK, ITEM_TILES, TILE), jnp.float32),
            pltpu.VMEM((GRAM_ROWS, TILE), jnp.float32),
            pltpu.VMEM((GRAM_ROWS, TILE), jnp.float32),
            pltpu.SMEM((GRAM_ROWS, TILE), jnp.float32),
            pltpu.SMEM((GRAM_ROWS, TILE), jnp.float32),
            pltpu.SemaphoreType.DMA((2,)),
        ],
        compiler_params=params(16),
        name="sweep",
    )(*parts)


def after(value, *others):
    return lax.optimization_barrier((value, others))[0]


def shards(tile_values, tile_rows, tile_cols, tile_patterns, tile_counts, factor):
    items, (order, starts) = lax.optimization_barrier(
        (spread(factor.T), plan(tile_rows, tile_cols, tile_counts))
    )
    a_head, a_tail, b_head, b_tail = arranged(items)
    a_line, b_line = laid(line(a_head, a_tail, 0), A_ROWS), laid(line(b_head, b_tail, 1), B_ROWS)
    tile_values = pltpu.with_memory_space_constraint(tile_values, pltpu.HBM)
    tiles = prepare(tile_counts, after(tile_patterns, a_line, b_line), tile_values)
    add = functools.partial(add_parts, order, starts, tiles)

    a_below, a_above = shift(a_line, 1, 1), shift(a_line, 1, -1)
    b_below, b_above = shift(b_line, 0, 1), shift(b_line, 0, -1)
    sums = add({0: a_line, 1: b_line}, None)
    a_below, a_above, b_below, b_above = (after(block, sums) for block in (a_below, a_above, b_below, b_above))
    cut = a_line.shape[0] // 2
    a_far = jnp.concatenate([shift(a_below[:cut], 1, 1), shift(a_above[cut:], 1, -1)])
    cut = b_line.shape[0] // 2
    b_far = jnp.concatenate([shift(b_below[:cut], 0, 1), shift(b_above[cut:], 0, -1)])
    sums = add({2: a_below, 4: a_above, 3: b_below, 5: b_above}, sums)
    sums = add({7: b_far, 9: b_far}, sums)
    sums = add({6: a_far}, sums)

    messages = deal(sums)
    others = [swap_cores(message) for message in messages]
    sums = add({8: a_far}, after(sums, *messages))
    own, up, across, down = joined(0, sums, others[0])
    sums = after(sums, own)
    passed = shift(across, 2, 1)
    own1, up1, across1, down1 = joined(1, sums, others[1])
    passed1, from_below = shift(across1, 2, -1), shift(up1, 2, 1)
    from_above = shift(after(down, own1), 2, -1)
    found = [own, passed, from_above, shift(onward(up, passed), 2, 1)]
    found += [own1, from_below, shift(onward(down1, passed1), 2, -1)]
    return sweep([factor.T] + found).T


def solution(mesh):
    spec = P(("row", "col"))
    return jax.shard_map(
        shards,
        mesh=mesh,
        in_specs=(P(("row", "col"), None, None), spec, spec, spec, spec, P(("row", "col"), None)),
        out_specs=P(("row", "col"), None),
        check_vma=False,
    )
```

time: 129 us -> 109 us (0.84)
  waiting for transfers between devices: 48.3 us -> 39.6 us
  Pallas kernels: 27.6 us -> 23 us
  starting transfers between devices: 46.3 us -> 42.9 us
  local copies, waits for them, and re-layouts: 2.07 us -> 0.23 us
    ppermute x23 -> x25, waiting for transfers between devices: 48.3 us -> 39.6 us  [permute(): lax.ppermute(array, AXES, [(d, number(*move(*coords(d)))) for d in range(...]
    ppermute x23 -> x25, starting transfers between devices: 46.3 us -> 42.9 us  [permute(): lax.ppermute(array, AXES, [(d, number(*move(*coords(d)))) for d in range(...]
    pallas_call x1, Pallas kernels: 9.71 us -> 7.48 us  [prepare(): pl.pallas_call(prepare_kernel, grid_spec=pltpu.PrefetchScalarGridSpec(num...]
    unnamed x12 -> x5, local copies, waits for them, and re-layouts: 1.86 us -> 0.05 us
    pallas_call x8 -> x14, Pallas kernels: 12.7 us -> 11.3 us  [the longest x5 9.73 us: add_parts(): pl.pallas_call(functools.partial(part_kernel, keys, sums is None), in_spe...]
  transfers between devices with their start and end apart: 23 -> 25, of which waited for: 10 -> 11; matrix products, arithmetic and copies ran while one was open for 2% -> 2% of each run, Pallas kernels for 14% -> 16%
where the time goes in v2:
time: 109 us
  starting transfers between devices  42.9 us (39%)
  waiting for transfers between devices  39.6 us (36%)
  Pallas kernels  23 us (21%)
  other arithmetic  2.14 us (2%)
    ppermute x25, starting transfers between devices, permute(): lax.ppermute(array, AXES, [(d, number(*move(*coords(d)))) for d in range(...  42.9 us
    ppermute x25, waiting for transfers between devices, permute(): lax.ppermute(array, AXES, [(d, number(*move(*coords(d)))) for d in range(...  39.6 us
    pallas_call x5, Pallas kernels, add_parts(): pl.pallas_call(functools.partial(part_kernel, keys, sums is None), in_spe...  9.73 us
    pallas_call x1, Pallas kernels, prepare(): pl.pallas_call(prepare_kernel, grid_spec=pltpu.PrefetchScalarGridSpec(num...  7.48 us
    pallas_call x1, Pallas kernels, sweep(): pl.pallas_call(sweep_kernel, in_specs=[WHOLE] * len(parts), out_specs=WHO...  4.13 us
  transfers between devices with their start and end apart: 25, of which 11 were waited for; matrix products, arithmetic and copies ran while one was open for 2% of the time, Pallas kernels for 16%

profile of v2, /device:TPU:0, one launch (start us, length us, event | category | flops | bytes accessed | tf_op | source)
XLA Modules:
  0.0 108.9 jit_solution(16745072455845139742)
XLA Ops:
  0.0 1.7 %collective-permute-start = (f32[64,2048]{1,0:T(8,128)}, f32[64,2048]{1,0:T(8,128)S(1)}, u32[]{:S(2)}, u32[]{:S(2)}) collective-permute-start(f32[64,2048]{1,0:T(8,128)} %bitcast.4), channel_id=1, source_target_pairs={{0,0},{1,88},{2,32},{3,120},{4,64},{5,24},{6,96},{7,56},{8,8},{9,8... | collective-permute-start | bytes 1572872 | tf_op jit(solution)/shard_map/ppermute | solution.py:41
  2.3 0.8 add_select_fusion.20
  3.1 0.1 convert_reduce_fusion.1.starts
  3.2 0.2 convert_reduce_fusion
  3.5 0.7 fusion.23
  4.2 0.2 select_reduce_fusion.order
  4.4 0.0 collective-permute-done.items_ref
  4.4 1.7 %collective-permute-start.5 = (f32[256,128]{1,0:T(8,128)S(1)}, f32[256,128]{1,0:T(8,128)S(1)}, u32[]{:S(2)}, u32[]{:S(2)}) collective-permute-start(f32[256,128]{1,0:T(8,128)S(1)} %get-tuple-element.33.refs_0_), channel_id=1, source_target_pairs={{0,8},{1,9},{2,10},{3,11},{4,12},{5,13},{6,14},{7,15},{8,0},{9,1},... | collective-permute-start | bytes 393224 | tf_op jit(solution)/shard_map/ppermute | solution.py:41
  6.1 11.5 %collective-permute-start.7 = (f32[256,128]{1,0:T(8,128)S(1)}, f32[256,128]{1,0:T(8,128)S(1)}, u32[]{:S(2)}, u32[]{:S(2)}) collective-permute-start(f32[256,128]{1,0:T(8,128)S(1)} %get-tuple-element.34.refs_3_), channel_id=1, source_target_pairs={{0,24},{1,25},{2,26},{3,27},{4,28},{5,29},{6,30},{7,31},{8,16},{9,... | collective-permute-start | bytes 393224 | tf_op jit(solution)/shard_map/ppermute | solution.py:41
  17.6 1.0 head.1.refs_0_
  18.6 3.4 %collective-permute-start.3 = (f32[256,128]{1,0:T(8,128)S(1)}, f32[256,128]{1,0:T(8,128)S(1)}, u32[]{:S(2)}, u32[]{:S(2)}) collective-permute-start(f32[256,128]{1,0:T(8,128)S(1)} %get-tuple-element.32.refs_3_), channel_id=1, source_target_pairs={{0,96},{1,97},{2,98},{3,99},{4,100},{5,101},{6,102},{7,103},{8,104... | collective-permute-start | bytes 393224 | tf_op jit(solution)/shard_map/ppermute | solution.py:41
  22.0 0.0 collective-permute-start.1
  22.0 0.0 collective-permute-done.5.refs_1_
  22.0 2.3 %collective-permute-start.6 = (f32[512,128]{1,0:T(8,128)S(1)}, f32[512,128]{1,0:T(8,128)S(1)}, u32[]{:S(2)}, u32[]{:S(2)}) collective-permute-start(f32[512,128]{1,0:T(8,128)S(1)} %pad_maximum_fusion.3), channel_id=1, source_target_pairs={{0,24},{1,25},{2,26},{3,27},{4,28},{5,29},{6,30},{7,31},{8,16},{9,... | collective-permute-start | bytes 786440 | tf_op jit(solution)/shard_map/ppermute | solution.py:41
  24.3 0.1 collective-permute-start.8
  24.4 2.7 %collective-permute-done.1.refs_1_ = f32[288,128]{1,0:T(8,128)S(1)} collective-permute-done((f32[288,128]{1,0:T(8,128)S(1)}, f32[288,128]{1,0:T(8,128)S(1)}, u32[]{:S(2)}, u32[]{:S(2)}) %collective-permute-start.1) | collective-permute-done | bytes 147488 | tf_op jit(solution)/shard_map/ppermute | solution.py:41
  27.2 0.2 collective-permute-start.2
  27.4 0.7 collective-permute-start.4
  28.1 2.7 %collective-permute-done.6.refs_2_ = f32[512,128]{1,0:T(8,128)S(1)} collective-permute-done((f32[512,128]{1,0:T(8,128)S(1)}, f32[512,128]{1,0:T(8,128)S(1)}, u32[]{:S(2)}, u32[]{:S(2)}) %collective-permute-start.6) | collective-permute-done | bytes 262176 | tf_op jit(solution)/shard_map/ppermute | solution.py:41
  30.8 0.0 collective-permute-done.8.refs_5_
  30.8 0.1 laid.3.refs_1_
  30.9 0.0 copy-start.1
  30.9 2.6 %collective-permute-start.15 = (f32[2048,128]{1,0:T(8,128)S(1)}, f32[2048,128]{1,0:T(8,128)S(1)}, u32[]{:S(2)}, u32[]{:S(2)}) collective-permute-start(f32[2048,128]{1,0:T(8,128)S(1)} %laid.3.refs_1_), channel_id=1, source_target_pairs={{0,96},{1,97},{2,98},{3,99},{4,100},{5,101},{6,102},{7,103},{8,104... | collective-permute-start | bytes 3145736 | tf_op jit(solution)/shard_map/ppermute | solution.py:41
  33.5 0.0 collective-permute-start.13
  33.5 2.2 %collective-permute-done.4.refs_5_ = f32[512,128]{1,0:T(8,128)S(1)} collective-permute-done((f32[512,128]{1,0:T(8,128)S(1)}, f32[512,128]{1,0:T(8,128)S(1)}, u32[]{:S(2)}, u32[]{:S(2)}) %collective-permute-start.4) | collective-permute-done | bytes 262176 | tf_op jit(solution)/shard_map/ppermute | solution.py:41
  35.8 0.1 laid.2.refs_0_
  35.8 2.2 %collective-permute-start.9 = (f32[2176,128]{1,0:T(8,128)S(1)}, f32[2176,128]{1,0:T(8,128)S(1)}, u32[]{:S(2)}, u32[]{:S(2)}) collective-permute-start(f32[2176,128]{1,0:T(8,128)S(1)} %laid.2.refs_0_), channel_id=1, source_target_pairs={{0,8},{1,9},{2,10},{3,11},{4,12},{5,13},{6,14},{7,15},{8,16},{9,17... | collective-permute-start | bytes 3342344 | tf_op jit(solution)/shard_map/ppermute | solution.py:41
  38.0 1.1 %collective-permute-start.11 = (f32[2176,128]{1,0:T(8,128)S(1)}, f32[2176,128]{1,0:T(8,128)S(1)}, u32[]{:S(2)}, u32[]{:S(2)}) collective-permute-start(f32[2176,128]{1,0:T(8,128)S(1)} %laid.2.refs_0_), channel_id=1, source_target_pairs={{0,24},{1,25},{2,26},{3,27},{4,28},{5,29},{6,30},{7,31},{8,0},{9,1... | collective-permute-start | bytes 3342344 | tf_op jit(solution)/shard_map/ppermute | solution.py:41
  39.1 7.5 %prepare.1.tiles_ref = bf16[320,256,128]{2,1,0:T(8,128)(2,1)S(1)} custom-call(s32[1]{0:T(128)} %copy.16.count, s32[320]{0:T(512)S(1)} %copy-done.1, f32[320,128,128]{2,1,0:T(8,128)} %values_ref.1), custom_call_target="tpu_custom_call" | custom-call | flops 1 | bytes 1 | tf_op jit(solution)/shard_map/prepare/pallas_call | solution.py:150
  46.6 2.6 %part.5.refs_4_ = f32[8288,128]{1,0:T(8,128)S(1)} custom-call(s32[336]{0:T(512)S(1)} %select_reduce_fusion.order, s32[11]{0:T(128)S(1)} %convert_reduce_fusion.1.starts, bf16[320,256,128]{2,1,0:T(8,128)(2,1)S(1)} %prepare.1.tiles_ref, f32[2176,128]{1,0:T(8,128)S(1)} %laid.2.refs_0_, f32[2048,128]{1,0:T(8,128)S(1)} %laid.3.refs_1_), custom_call_target="tpu_custom_call" | custom-call | flops 1 | bytes 1 | tf_op jit(solution)/shard_map/part/pallas_call | solution.py:241
  49.3 7.0 %collective-permute-done.15.refs_3_ = f32[2048,128]{1,0:T(8,128)S(1)} collective-permute-done((f32[2048,128]{1,0:T(8,128)S(1)}, f32[2048,128]{1,0:T(8,128)S(1)}, u32[]{:S(2)}, u32[]{:S(2)}) %collective-permute-start.15) | collective-permute-done | bytes 1048608 | tf_op jit(solution)/shard_map/ppermute | solution.py:41
  56.3 2.5 %collective-permute-done.13.refs_1_ = f32[2048,128]{1,0:T(8,128)S(1)} collective-permute-done((f32[2048,128]{1,0:T(8,128)S(1)}, f32[2048,128]{1,0:T(8,128)S(1)}, u32[]{:S(2)}, u32[]{:S(2)}) %collective-permute-start.13) | collective-permute-done | bytes 1048608 | tf_op jit(solution)/shard_map/ppermute | solution.py:41
  58.9 0.1 collective-permute-start.14
  58.9 3.2 %collective-permute-start.16 = (f32[1024,128]{1,0:T(8,128)S(1)}, f32[1024,128]{1,0:T(8,128)S(1)}, u32[]{:S(2)}, u32[]{:S(2)}) collective-permute-start(f32[1024,128]{1,0:T(8,128)S(1)} %slice.15), channel_id=1, source_target_pairs={{0,96},{1,97},{2,98},{3,99},{4,100},{5,101},{6,102},{7,103},{8,104... | collective-permute-start | bytes 1572872 | tf_op jit(solution)/shard_map/ppermute | solution.py:41
  62.2 0.0 collective-permute-done.9.refs_0_
  62.2 0.3 collective-permute-start.10
  62.5 3.1 %collective-permute-start.12 = (f32[1088,128]{1,0:T(8,128)S(1)}, f32[1088,128]{1,0:T(8,128)S(1)}, u32[]{:S(2)}, u32[]{:S(2)}) collective-permute-start(f32[1088,128]{1,0:T(8,128)S(1)} %slice.13), channel_id=1, source_target_pairs={{0,24},{1,25},{2,26},{3,27},{4,28},{5,29},{6,30},{7,31},{8,0},{9,1... | collective-permute-start | bytes 1671176 | tf_op jit(solution)/shard_map/ppermute | solution.py:41
  65.6 3.9 %part.6.refs_2_ = f32[8288,128]{1,0:T(8,128)S(1)} custom-call(s32[336]{0:T(512)S(1)} %select_reduce_fusion.order, s32[11]{0:T(128)S(1)} %convert_reduce_fusion.1.starts, bf16[320,256,128]{2,1,0:T(8,128)(2,1)S(1)} %prepare.1.tiles_ref, f32[2176,128]{1,0:T(8,128)S(1)} %collective-permute-done.9.refs_0_, ...), custom_call_target="tpu_custom_call", output_to_operand_aliasing={{}: (7, {})} | custom-call | flops 1 | bytes 1 | tf_op jit(solution)/shard_map/part/pallas_call | solution.py:241
  69.5 2.6 %collective-permute-done.14 = f32[1024,128]{1,0:T(8,128)S(1)} collective-permute-done((f32[1024,128]{1,0:T(8,128)S(1)}, f32[1024,128]{1,0:T(8,128)S(1)}, u32[]{:S(2)}, u32[]{:S(2)}) %collective-permute-start.14) | collective-permute-done | bytes 524320 | tf_op jit(solution)/shard_map/ppermute | solution.py:41
  72.1 0.0 collective-permute-done.16
  72.1 0.1 pad_maximum_fusion.refs_0_.refs_1_
  72.1 1.5 %part.7.refs_1_ = f32[8288,128]{1,0:T(8,128)S(1)} custom-call(s32[336]{0:T(512)S(1)} %select_reduce_fusion.order, s32[11]{0:T(128)S(1)} %convert_reduce_fusion.1.starts, bf16[320,256,128]{2,1,0:T(8,128)(2,1)S(1)} %prepare.1.tiles_ref, f32[2048,128]{1,0:T(8,128)S(1)} %pad_maximum_fusion.refs_0_.refs_1_, ...), custom_call_target="tpu_custom_call", output_to_operand_aliasing={{}: (5, {})} | custom-call | flops 1 | bytes 1 | tf_op jit(solution)/shard_map/part/pallas_call | solution.py:241
  73.6 1.9 %collective-permute-done.10 = f32[1088,128]{1,0:T(8,128)S(1)} collective-permute-done((f32[1088,128]{1,0:T(8,128)S(1)}, f32[1088,128]{1,0:T(8,128)S(1)}, u32[]{:S(2)}, u32[]{:S(2)}) %collective-permute-start.10) | collective-permute-done | bytes 557088 | tf_op jit(solution)/shard_map/ppermute | solution.py:41
  75.6 0.9 part.8.sums_ref.refs_1_
  76.5 0.1 deal.1
  76.7 0.1 collective-permute-start.17
  76.8 0.5 collective-permute-start.19
  77.3 0.9 part.9.sums_ref
  78.1 1.3 %collective-permute-done.17.other_ref = f32[2080,128]{1,0:T(8,128)S(1)} collective-permute-done((f32[2080,128]{1,0:T(8,128)S(1)}, f32[2080,128]{1,0:T(8,128)S(1)}, u32[]{:S(2)}, u32[]{:S(2)}) %collective-permute-start.17) | collective-permute-done | bytes 1064992 | tf_op jit(solution)/shard_map/ppermute | solution.py:41
  79.4 0.1 joined.2
  79.6 1.7 %collective-permute-start.18 = (f32[544,128]{1,0:T(8,128)S(1)}, f32[544,128]{1,0:T(8,128)S(1)}, u32[]{:S(2)}, u32[]{:S(2)}) collective-permute-start(f32[544,128]{1,0:T(8,128)S(1)} %get-tuple-element.44), channel_id=1, source_target_pairs={{0,2},{1,3},{2,4},{3,5},{4,6},{5,7},{6,0},{7,1},{8,10},{9,11},{10,... | collective-permute-start | bytes 835592 | tf_op jit(solution)/shard_map/ppermute | solution.py:41
  81.3 0.0 collective-permute-done.19.other_ref
  81.3 0.1 joined.3
  81.4 0.0 copy-start
  81.4 1.9 %collective-permute-start.23 = (f32[512,128]{1,0:T(8,128)S(1)}, f32[512,128]{1,0:T(8,128)S(1)}, u32[]{:S(2)}, u32[]{:S(2)}) collective-permute-start(f32[512,128]{1,0:T(8,128)S(1)} %get-tuple-element.52), channel_id=1, source_target_pairs={{0,6},{1,7},{2,0},{3,1},{4,2},{5,3},{6,4},{7,5},{8,14},{9,15},{10,... | collective-permute-start | bytes 786440 | tf_op jit(solution)/shard_map/ppermute | solution.py:41
  83.3 0.7 collective-permute-start.20
  83.9 5.8 %collective-permute-done.18.passed_ref.refs_2_ = f32[544,128]{1,0:T(8,128)S(1)} collective-permute-done((f32[544,128]{1,0:T(8,128)S(1)}, f32[544,128]{1,0:T(8,128)S(1)}, u32[]{:S(2)}, u32[]{:S(2)}) %collective-permute-start.18) | collective-permute-done | bytes 278560 | tf_op jit(solution)/shard_map/ppermute | solution.py:41
  89.8 0.3 collective-permute-start.21
  90.1 0.5 collective-permute-start.22
  90.6 0.1 collective-permute-done.23.passed_ref
  90.7 3.1 %collective-permute-start.24 = (f32[512,128]{1,0:T(8,128)S(1)}, f32[512,128]{1,0:T(8,128)S(1)}, u32[]{:S(2)}, u32[]{:S(2)}) collective-permute-start(f32[512,128]{1,0:T(8,128)S(1)} %onward.3), channel_id=1, source_target_pairs={{0,6},{1,7},{2,0},{3,1},{4,2},{5,3},{6,4},{7,5},{8,14},{9,15},{10,... | collective-permute-start | bytes 786440 | tf_op jit(solution)/shard_map/ppermute | solution.py:41
  93.8 10.8 %collective-permute-done.22.refs_6_ = f32[512,128]{1,0:T(8,128)S(1)} collective-permute-done((f32[512,128]{1,0:T(8,128)S(1)}, f32[512,128]{1,0:T(8,128)S(1)}, u32[]{:S(2)}, u32[]{:S(2)}) %collective-permute-start.22) | collective-permute-done | bytes 262176 | tf_op jit(solution)/shard_map/ppermute | solution.py:41
  104.5 0.0 collective-permute-done.21.refs_4_
  104.6 4.1 %sweep.1 = f32[64,2048]{1,0:T(8,128)} custom-call(f32[64,2048]{1,0:T(8,128)S(1)} %bitcast.5, f32[544,128]{1,0:T(8,128)S(1)} %get-tuple-element.43.refs_1_, f32[544,128]{1,0:T(8,128)S(1)} %collective-permute-done.18.passed_ref.refs_2_, f32[544,128]{1,0:T(8,128)S(1)} %collective-permute-done.20.refs_3_, f32[544,128]{1,0:T(8,128)S(1)} %collective-permute-done.21.refs_4_, ...), custom_call_target="tpu_custom_call" | custom-call | tf_op jit(solution)/shard_map/sweep/pallas_call | solution.py:386
  (22 shorter events, 0.4 us)
Async XLA Ops:
  0.0 4.4 %collective-permute-start = (f32[64,2048]{1,0:T(8,128)}, f32[64,2048]{1,0:T(8,128)S(1)}, u32[]{:S(2)}, u32[]{:S(2)}) collective-permute-start(f32[64,2048]{1,0:T(8,128)} %bitcast.4), channel_id=1, source_target_pairs={{0,0},{1,88},{2,32},{3,120},{4,64},{5,24},{6,96},{7,56},{8,8},{9,8... | collective-permute-start | bytes 1572872 | tf_op jit(solution)/shard_map/ppermute | solution.py:41
  4.4 17.6 %collective-permute-start.5 = (f32[256,128]{1,0:T(8,128)S(1)}, f32[256,128]{1,0:T(8,128)S(1)}, u32[]{:S(2)}, u32[]{:S(2)}) collective-permute-start(f32[256,128]{1,0:T(8,128)S(1)} %get-tuple-element.33.refs_0_), channel_id=1, source_target_pairs={{0,8},{1,9},{2,10},{3,11},{4,12},{5,13},{6,14},{7,15},{8,0},{9,1},... | collective-permute-start | bytes 393224 | tf_op jit(solution)/shard_map/ppermute | solution.py:41
  6.1 18.2 %collective-permute-start.7 = (f32[256,128]{1,0:T(8,128)S(1)}, f32[256,128]{1,0:T(8,128)S(1)}, u32[]{:S(2)}, u32[]{:S(2)}) collective-permute-start(f32[256,128]{1,0:T(8,128)S(1)} %get-tuple-element.34.refs_3_), channel_id=1, source_target_pairs={{0,24},{1,25},{2,26},{3,27},{4,28},{5,29},{6,30},{7,31},{8,16},{9,... | collective-permute-start | bytes 393224 | tf_op jit(solution)/shard_map/ppermute | solution.py:41
  18.6 8.7 %collective-permute-start.3 = (f32[256,128]{1,0:T(8,128)S(1)}, f32[256,128]{1,0:T(8,128)S(1)}, u32[]{:S(2)}, u32[]{:S(2)}) collective-permute-start(f32[256,128]{1,0:T(8,128)S(1)} %get-tuple-element.32.refs_3_), channel_id=1, source_target_pairs={{0,96},{1,97},{2,98},{3,99},{4,100},{5,101},{6,102},{7,103},{8,104... | collective-permute-start | bytes 393224 | tf_op jit(solution)/shard_map/ppermute | solution.py:41
  22.0 5.1 %collective-permute-start.1 = (f32[288,128]{1,0:T(8,128)S(1)}, f32[288,128]{1,0:T(8,128)S(1)}, u32[]{:S(2)}, u32[]{:S(2)}) collective-permute-start(f32[288,128]{1,0:T(8,128)S(1)} %head.1.refs_0_), channel_id=1, source_target_pairs={{0,32},{1,33},{2,34},{3,35},{4,36},{5,37},{6,38},{7,39},{8,40},{9,... | collective-permute-start | bytes 442376 | tf_op jit(solution)/shard_map/ppermute | solution.py:41
  22.0 8.8 %collective-permute-start.6 = (f32[512,128]{1,0:T(8,128)S(1)}, f32[512,128]{1,0:T(8,128)S(1)}, u32[]{:S(2)}, u32[]{:S(2)}) collective-permute-start(f32[512,128]{1,0:T(8,128)S(1)} %pad_maximum_fusion.3), channel_id=1, source_target_pairs={{0,24},{1,25},{2,26},{3,27},{4,28},{5,29},{6,30},{7,31},{8,16},{9,... | collective-permute-start | bytes 786440 | tf_op jit(solution)/shard_map/ppermute | solution.py:41
  24.3 6.5 %collective-permute-start.8 = (f32[512,128]{1,0:T(8,128)S(1)}, f32[512,128]{1,0:T(8,128)S(1)}, u32[]{:S(2)}, u32[]{:S(2)}) collective-permute-start(f32[512,128]{1,0:T(8,128)S(1)} %pad_maximum_fusion.4), channel_id=1, source_target_pairs={{0,8},{1,9},{2,10},{3,11},{4,12},{5,13},{6,14},{7,15},{8,0},{9,1},... | collective-permute-start | bytes 786440 | tf_op jit(solution)/shard_map/ppermute | solution.py:41
  27.2 8.6 %collective-permute-start.2 = (f32[576,128]{1,0:T(8,128)S(1)}, f32[576,128]{1,0:T(8,128)S(1)}, u32[]{:S(2)}, u32[]{:S(2)}) collective-permute-start(f32[576,128]{1,0:T(8,128)S(1)} %pad_maximum_fusion.1), channel_id=1, source_target_pairs={{0,96},{1,97},{2,98},{3,99},{4,100},{5,101},{6,102},{7,103},{8,104... | collective-permute-start | bytes 884744 | tf_op jit(solution)/shard_map/ppermute | solution.py:41
  27.4 8.4 %collective-permute-start.4 = (f32[512,128]{1,0:T(8,128)S(1)}, f32[512,128]{1,0:T(8,128)S(1)}, u32[]{:S(2)}, u32[]{:S(2)}) collective-permute-start(f32[512,128]{1,0:T(8,128)S(1)} %pad_maximum_fusion.2), channel_id=1, source_target_pairs={{0,32},{1,33},{2,34},{3,35},{4,36},{5,37},{6,38},{7,39},{8,40},{9,... | collective-permute-start | bytes 786440 | tf_op jit(solution)/shard_map/ppermute | solution.py:41
  30.9 8.3 %copy-start.1 = (s32[320]{0:T(512)S(1)}, s32[320]{0:T(512)}, u32[]{:S(2)}) copy-start(s32[320]{0:T(512)} %patterns) | copy-start | bytes 3844
  30.9 25.4 %collective-permute-start.15 = (f32[2048,128]{1,0:T(8,128)S(1)}, f32[2048,128]{1,0:T(8,128)S(1)}, u32[]{:S(2)}, u32[]{:S(2)}) collective-permute-start(f32[2048,128]{1,0:T(8,128)S(1)} %laid.3.refs_1_), channel_id=1, source_target_pairs={{0,96},{1,97},{2,98},{3,99},{4,100},{5,101},{6,102},{7,103},{8,104... | collective-permute-start | bytes 3145736 | tf_op jit(solution)/shard_map/ppermute | solution.py:41
  33.5 25.3 %collective-permute-start.13 = (f32[2048,128]{1,0:T(8,128)S(1)}, f32[2048,128]{1,0:T(8,128)S(1)}, u32[]{:S(2)}, u32[]{:S(2)}) collective-permute-start(f32[2048,128]{1,0:T(8,128)S(1)} %laid.3.refs_1_), channel_id=1, source_target_pairs={{0,32},{1,33},{2,34},{3,35},{4,36},{5,37},{6,38},{7,39},{8,40},{9,... | collective-permute-start | bytes 3145736 | tf_op jit(solution)/shard_map/ppermute | solution.py:41
  35.8 26.3 %collective-permute-start.9 = (f32[2176,128]{1,0:T(8,128)S(1)}, f32[2176,128]{1,0:T(8,128)S(1)}, u32[]{:S(2)}, u32[]{:S(2)}) collective-permute-start(f32[2176,128]{1,0:T(8,128)S(1)} %laid.2.refs_0_), channel_id=1, source_target_pairs={{0,8},{1,9},{2,10},{3,11},{4,12},{5,13},{6,14},{7,15},{8,16},{9,17... | collective-permute-start | bytes 3342344 | tf_op jit(solution)/shard_map/ppermute | solution.py:41
  38.0 24.5 %collective-permute-start.11 = (f32[2176,128]{1,0:T(8,128)S(1)}, f32[2176,128]{1,0:T(8,128)S(1)}, u32[]{:S(2)}, u32[]{:S(2)}) collective-permute-start(f32[2176,128]{1,0:T(8,128)S(1)} %laid.2.refs_0_), channel_id=1, source_target_pairs={{0,24},{1,25},{2,26},{3,27},{4,28},{5,29},{6,30},{7,31},{8,0},{9,1... | collective-permute-start | bytes 3342344 | tf_op jit(solution)/shard_map/ppermute | solution.py:41
  58.9 13.2 %collective-permute-start.14 = (f32[1024,128]{1,0:T(8,128)S(1)}, f32[1024,128]{1,0:T(8,128)S(1)}, u32[]{:S(2)}, u32[]{:S(2)}) collective-permute-start(f32[1024,128]{1,0:T(8,128)S(1)} %slice.14), channel_id=1, source_target_pairs={{0,32},{1,33},{2,34},{3,35},{4,36},{5,37},{6,38},{7,39},{8,40},{9,... | collective-permute-start | bytes 1572872 | tf_op jit(solution)/shard_map/ppermute | solution.py:41
  58.9 13.1 %collective-permute-start.16 = (f32[1024,128]{1,0:T(8,128)S(1)}, f32[1024,128]{1,0:T(8,128)S(1)}, u32[]{:S(2)}, u32[]{:S(2)}) collective-permute-start(f32[1024,128]{1,0:T(8,128)S(1)} %slice.15), channel_id=1, source_target_pairs={{0,96},{1,97},{2,98},{3,99},{4,100},{5,101},{6,102},{7,103},{8,104... | collective-permute-start | bytes 1572872 | tf_op jit(solution)/shard_map/ppermute | solution.py:41
  62.2 13.3 %collective-permute-start.10 = (f32[1088,128]{1,0:T(8,128)S(1)}, f32[1088,128]{1,0:T(8,128)S(1)}, u32[]{:S(2)}, u32[]{:S(2)}) collective-permute-start(f32[1088,128]{1,0:T(8,128)S(1)} %slice.12), channel_id=1, source_target_pairs={{0,8},{1,9},{2,10},{3,11},{4,12},{5,13},{6,14},{7,15},{8,16},{9,17... | collective-permute-start | bytes 1671176 | tf_op jit(solution)/shard_map/ppermute | solution.py:41
  62.5 13.1 %collective-permute-start.12 = (f32[1088,128]{1,0:T(8,128)S(1)}, f32[1088,128]{1,0:T(8,128)S(1)}, u32[]{:S(2)}, u32[]{:S(2)}) collective-permute-start(f32[1088,128]{1,0:T(8,128)S(1)} %slice.13), channel_id=1, source_target_pairs={{0,24},{1,25},{2,26},{3,27},{4,28},{5,29},{6,30},{7,31},{8,0},{9,1... | collective-permute-start | bytes 1671176 | tf_op jit(solution)/shard_map/ppermute | solution.py:41
  76.7 2.8 %collective-permute-start.17 = (f32[2080,128]{1,0:T(8,128)S(1)}, f32[2080,128]{1,0:T(8,128)S(1)}, u32[]{:S(2)}, u32[]{:S(2)}) collective-permute-start(f32[2080,128]{1,0:T(8,128)S(1)} %get-tuple-element.40), channel_id=1, source_target_pairs={{0,1},{1,0},{2,3},{3,2},{4,5},{5,4},{6,7},{7,6},{8,9},{9,8},{10,11... | collective-permute-start | bytes 3194888 | tf_op jit(solution)/shard_map/ppermute | solution.py:41
  76.8 4.5 %collective-permute-start.19 = (f32[2048,128]{1,0:T(8,128)S(1)}, f32[2048,128]{1,0:T(8,128)S(1)}, u32[]{:S(2)}, u32[]{:S(2)}) collective-permute-start(f32[2048,128]{1,0:T(8,128)S(1)} %get-tuple-element.41), channel_id=1, source_target_pairs={{0,1},{1,0},{2,3},{3,2},{4,5},{5,4},{6,7},{7,6},{8,9},{9,8},{10,11... | collective-permute-start | bytes 3145736 | tf_op jit(solution)/shard_map/ppermute | solution.py:41
  79.6 10.2 %collective-permute-start.18 = (f32[544,128]{1,0:T(8,128)S(1)}, f32[544,128]{1,0:T(8,128)S(1)}, u32[]{:S(2)}, u32[]{:S(2)}) collective-permute-start(f32[544,128]{1,0:T(8,128)S(1)} %get-tuple-element.44), channel_id=1, source_target_pairs={{0,2},{1,3},{2,4},{3,5},{4,6},{5,7},{6,0},{7,1},{8,10},{9,11},{10,... | collective-permute-start | bytes 835592 | tf_op jit(solution)/shard_map/ppermute | solution.py:41
  81.4 23.2 %copy-start = (f32[2048,64]{0,1:T(8,128)S(1)}, f32[2048,64]{0,1:T(8,128)}, u32[]{:S(2)}) copy-start(f32[2048,64]{0,1:T(8,128)} %param.11) | copy-start | bytes 1572868
  81.4 9.3 %collective-permute-start.23 = (f32[512,128]{1,0:T(8,128)S(1)}, f32[512,128]{1,0:T(8,128)S(1)}, u32[]{:S(2)}, u32[]{:S(2)}) collective-permute-start(f32[512,128]{1,0:T(8,128)S(1)} %get-tuple-element.52), channel_id=1, source_target_pairs={{0,6},{1,7},{2,0},{3,1},{4,2},{5,3},{6,4},{7,5},{8,14},{9,15},{10,... | collective-permute-start | bytes 786440 | tf_op jit(solution)/shard_map/ppermute | solution.py:41
  83.3 21.3 %collective-permute-start.20 = (f32[544,128]{1,0:T(8,128)S(1)}, f32[544,128]{1,0:T(8,128)S(1)}, u32[]{:S(2)}, u32[]{:S(2)}) collective-permute-start(f32[544,128]{1,0:T(8,128)S(1)} %get-tuple-element.48), channel_id=1, source_target_pairs={{0,6},{1,7},{2,0},{3,1},{4,2},{5,3},{6,4},{7,5},{8,14},{9,15},{10,... | collective-permute-start | bytes 835592 | tf_op jit(solution)/shard_map/ppermute | solution.py:41
  89.8 14.8 %collective-permute-start.21 = (f32[544,128]{1,0:T(8,128)S(1)}, f32[544,128]{1,0:T(8,128)S(1)}, u32[]{:S(2)}, u32[]{:S(2)}) collective-permute-start(f32[544,128]{1,0:T(8,128)S(1)} %onward.2), channel_id=1, source_target_pairs={{0,2},{1,3},{2,4},{3,5},{4,6},{5,7},{6,0},{7,1},{8,10},{9,11},{10,... | collective-permute-start | bytes 835592 | tf_op jit(solution)/shard_map/ppermute | solution.py:41
  90.1 14.5 %collective-permute-start.22 = (f32[512,128]{1,0:T(8,128)S(1)}, f32[512,128]{1,0:T(8,128)S(1)}, u32[]{:S(2)}, u32[]{:S(2)}) collective-permute-start(f32[512,128]{1,0:T(8,128)S(1)} %get-tuple-element.50), channel_id=1, source_target_pairs={{0,2},{1,3},{2,4},{3,5},{4,6},{5,7},{6,0},{7,1},{8,10},{9,11},{10,... | collective-permute-start | bytes 786440 | tf_op jit(solution)/shard_map/ppermute | solution.py:41
  90.7 13.8 %collective-permute-start.24 = (f32[512,128]{1,0:T(8,128)S(1)}, f32[512,128]{1,0:T(8,128)S(1)}, u32[]{:S(2)}, u32[]{:S(2)}) collective-permute-start(f32[512,128]{1,0:T(8,128)S(1)} %onward.3), channel_id=1, source_target_pairs={{0,6},{1,7},{2,0},{3,1},{4,2},{5,3},{6,4},{7,5},{8,14},{9,15},{10,... | collective-permute-start | bytes 786440 | tf_op jit(solution)/shard_map/ppermute | solution.py:41

commit v3 on v2

--- a/solution.py
+++ b/solution.py
@@ -15,7 +15,7 @@
 ITEM_TILES = 16
 ROW_TILES = 128
 DUMMY = ROW_TILES
-UNROLL = 8
+UNROLL = 16
 BATCH = 32
 A_ROWS = (HALF * RANK // 2 + GRAM_ROWS, HALF * RANK // 2)
 B_ROWS = (HALF * RANK // 2, HALF * RANK // 2)

time: 109 us -> 110 us (level)
  Pallas kernels: 23 us -> 32.9 us
  waiting for transfers between devices: 39.6 us -> 31.6 us
  starting transfers between devices: 42.9 us -> 41.5 us
    ppermute x25, waiting for transfers between devices: 39.6 us -> 31.6 us  [permute(): lax.ppermute(array, AXES, [(d, number(*move(*coords(d)))) for d in range(...]
    pallas_call x1, Pallas kernels: 7.48 us -> 13 us  [prepare(): pl.pallas_call(prepare_kernel, grid_spec=pltpu.PrefetchScalarGridSpec(num...]
    pallas_call x5, Pallas kernels: 9.73 us -> 14.2 us  [add_parts(): pl.pallas_call(functools.partial(part_kernel, keys, sums is None), in_spe...]
    ppermute x25, starting transfers between devices: 42.9 us -> 41.5 us  [permute(): lax.ppermute(array, AXES, [(d, number(*move(*coords(d)))) for d in range(...]
  transfers between devices with their start and end apart: 25 -> 25, of which waited for: 11 -> 12; matrix products, arithmetic and copies ran while one was open for 2% -> 2% of each run, Pallas kernels for 16% -> 25%
where the time goes in v3:
time: 110 us; the launch traced here: 109 us
  starting transfers between devices  41.5 us (38%)
  Pallas kernels  32.9 us (30%)
  waiting for transfers between devices  31.6 us (29%)
  other arithmetic  2.14 us (2%)
    ppermute x25, starting transfers between devices, permute(): lax.ppermute(array, AXES, [(d, number(*move(*coords(d)))) for d in range(...  41.5 us
    ppermute x25, waiting for transfers between devices, permute(): lax.ppermute(array, AXES, [(d, number(*move(*coords(d)))) for d in range(...  31.6 us
    pallas_call x5, Pallas kernels, add_parts(): pl.pallas_call(functools.partial(part_kernel, keys, sums is None), in_spe...  14.2 us
    pallas_call x1, Pallas kernels, prepare(): pl.pallas_call(prepare_kernel, grid_spec=pltpu.PrefetchScalarGridSpec(num...  13 us
    pallas_call x1, Pallas kernels, sweep(): pl.pallas_call(sweep_kernel, in_specs=[WHOLE] * len(parts), out_specs=WHO...  4.13 us
  transfers between devices with their start and end apart: 25, of which 12 were waited for; matrix products, arithmetic and copies ran while one was open for 2% of the time, Pallas kernels for 25%

profile of v3, /device:TPU:0, one launch (start us, length us, event | category | flops | bytes accessed | tf_op | source)
XLA Modules:
  0.0 109.4 jit_solution(11651468818074502852)
XLA Ops:
  0.0 1.7 %collective-permute-start = (f32[64,2048]{1,0:T(8,128)}, f32[64,2048]{1,0:T(8,128)S(1)}, u32[]{:S(2)}, u32[]{:S(2)}) collective-permute-start(f32[64,2048]{1,0:T(8,128)} %bitcast.4), channel_id=1, source_target_pairs={{0,0},{1,88},{2,32},{3,120},{4,64},{5,24},{6,96},{7,56},{8,8},{9,8... | collective-permute-start | bytes 1572872 | tf_op jit(solution)/shard_map/ppermute | solution.py:41
  2.3 0.8 add_select_fusion.20
  3.1 0.1 convert_reduce_fusion.1.starts
  3.2 0.2 convert_reduce_fusion
  3.5 0.7 fusion.23
  4.2 0.2 select_reduce_fusion.order
  4.4 0.0 collective-permute-done.items_ref
  4.4 1.7 %collective-permute-start.5 = (f32[256,128]{1,0:T(8,128)S(1)}, f32[256,128]{1,0:T(8,128)S(1)}, u32[]{:S(2)}, u32[]{:S(2)}) collective-permute-start(f32[256,128]{1,0:T(8,128)S(1)} %get-tuple-element.33.refs_0_), channel_id=1, source_target_pairs={{0,8},{1,9},{2,10},{3,11},{4,12},{5,13},{6,14},{7,15},{8,0},{9,1},... | collective-permute-start | bytes 393224 | tf_op jit(solution)/shard_map/ppermute | solution.py:41
  6.1 11.5 %collective-permute-start.7 = (f32[256,128]{1,0:T(8,128)S(1)}, f32[256,128]{1,0:T(8,128)S(1)}, u32[]{:S(2)}, u32[]{:S(2)}) collective-permute-start(f32[256,128]{1,0:T(8,128)S(1)} %get-tuple-element.34.refs_3_), channel_id=1, source_target_pairs={{0,24},{1,25},{2,26},{3,27},{4,28},{5,29},{6,30},{7,31},{8,16},{9,... | collective-permute-start | bytes 393224 | tf_op jit(solution)/shard_map/ppermute | solution.py:41
  17.6 1.0 head.1.refs_0_
  18.6 3.4 %collective-permute-start.3 = (f32[256,128]{1,0:T(8,128)S(1)}, f32[256,128]{1,0:T(8,128)S(1)}, u32[]{:S(2)}, u32[]{:S(2)}) collective-permute-start(f32[256,128]{1,0:T(8,128)S(1)} %get-tuple-element.32.refs_3_), channel_id=1, source_target_pairs={{0,96},{1,97},{2,98},{3,99},{4,100},{5,101},{6,102},{7,103},{8,104... | collective-permute-start | bytes 393224 | tf_op jit(solution)/shard_map/ppermute | solution.py:41
  22.0 0.0 collective-permute-start.1
  22.0 0.0 collective-permute-done.5.refs_1_
  22.0 2.3 %collective-permute-start.6 = (f32[512,128]{1,0:T(8,128)S(1)}, f32[512,128]{1,0:T(8,128)S(1)}, u32[]{:S(2)}, u32[]{:S(2)}) collective-permute-start(f32[512,128]{1,0:T(8,128)S(1)} %pad_maximum_fusion.3), channel_id=1, source_target_pairs={{0,24},{1,25},{2,26},{3,27},{4,28},{5,29},{6,30},{7,31},{8,16},{9,... | collective-permute-start | bytes 786440 | tf_op jit(solution)/shard_map/ppermute | solution.py:41
  24.3 0.0 collective-permute-done.7.refs_4_
  24.3 0.1 collective-permute-start.8
  24.4 2.7 %collective-permute-done.1.refs_1_ = f32[288,128]{1,0:T(8,128)S(1)} collective-permute-done((f32[288,128]{1,0:T(8,128)S(1)}, f32[288,128]{1,0:T(8,128)S(1)}, u32[]{:S(2)}, u32[]{:S(2)}) %collective-permute-start.1) | collective-permute-done | bytes 147488 | tf_op jit(solution)/shard_map/ppermute | solution.py:41
  27.2 0.2 collective-permute-start.2
  27.3 0.0 collective-permute-done.3.refs_4_
  27.4 0.7 collective-permute-start.4
  28.1 2.7 %collective-permute-done.6.refs_2_ = f32[512,128]{1,0:T(8,128)S(1)} collective-permute-done((f32[512,128]{1,0:T(8,128)S(1)}, f32[512,128]{1,0:T(8,128)S(1)}, u32[]{:S(2)}, u32[]{:S(2)}) %collective-permute-start.6) | collective-permute-done | bytes 262176 | tf_op jit(solution)/shard_map/ppermute | solution.py:41
  30.8 0.1 laid.3.refs_1_
  30.9 0.0 copy-start.1
  30.9 2.6 %collective-permute-start.15 = (f32[2048,128]{1,0:T(8,128)S(1)}, f32[2048,128]{1,0:T(8,128)S(1)}, u32[]{:S(2)}, u32[]{:S(2)}) collective-permute-start(f32[2048,128]{1,0:T(8,128)S(1)} %laid.3.refs_1_), channel_id=1, source_target_pairs={{0,96},{1,97},{2,98},{3,99},{4,100},{5,101},{6,102},{7,103},{8,104... | collective-permute-start | bytes 3145736 | tf_op jit(solution)/shard_map/ppermute | solution.py:41
  33.5 2.2 %collective-permute-done.4.refs_5_ = f32[512,128]{1,0:T(8,128)S(1)} collective-permute-done((f32[512,128]{1,0:T(8,128)S(1)}, f32[512,128]{1,0:T(8,128)S(1)}, u32[]{:S(2)}, u32[]{:S(2)}) %collective-permute-start.4) | collective-permute-done | bytes 262176 | tf_op jit(solution)/shard_map/ppermute | solution.py:41
  35.8 0.1 laid.2.refs_0_
  35.8 2.2 %collective-permute-start.9 = (f32[2176,128]{1,0:T(8,128)S(1)}, f32[2176,128]{1,0:T(8,128)S(1)}, u32[]{:S(2)}, u32[]{:S(2)}) collective-permute-start(f32[2176,128]{1,0:T(8,128)S(1)} %laid.2.refs_0_), channel_id=1, source_target_pairs={{0,8},{1,9},{2,10},{3,11},{4,12},{5,13},{6,14},{7,15},{8,16},{9,17... | collective-permute-start | bytes 3342344 | tf_op jit(solution)/shard_map/ppermute | solution.py:41
  38.0 1.1 %collective-permute-start.11 = (f32[2176,128]{1,0:T(8,128)S(1)}, f32[2176,128]{1,0:T(8,128)S(1)}, u32[]{:S(2)}, u32[]{:S(2)}) collective-permute-start(f32[2176,128]{1,0:T(8,128)S(1)} %laid.2.refs_0_), channel_id=1, source_target_pairs={{0,24},{1,25},{2,26},{3,27},{4,28},{5,29},{6,30},{7,31},{8,0},{9,1... | collective-permute-start | bytes 3342344 | tf_op jit(solution)/shard_map/ppermute | solution.py:41
  39.1 13.0 %prepare.1.tiles_ref = bf16[320,256,128]{2,1,0:T(8,128)(2,1)S(1)} custom-call(s32[1]{0:T(128)} %copy.16.count, s32[320]{0:T(512)S(1)} %copy-done.1, f32[320,128,128]{2,1,0:T(8,128)} %values_ref.1), custom_call_target="tpu_custom_call" | custom-call | flops 1 | bytes 1 | tf_op jit(solution)/shard_map/prepare/pallas_call | solution.py:150
  52.1 3.9 %part.5.refs_4_ = f32[8288,128]{1,0:T(8,128)S(1)} custom-call(s32[352]{0:T(512)S(1)} %select_reduce_fusion.order, s32[11]{0:T(128)S(1)} %convert_reduce_fusion.1.starts, bf16[320,256,128]{2,1,0:T(8,128)(2,1)S(1)} %prepare.1.tiles_ref, f32[2176,128]{1,0:T(8,128)S(1)} %laid.2.refs_0_, f32[2048,128]{1,0:T(8,128)S(1)} %laid.3.refs_1_), custom_call_target="tpu_custom_call" | custom-call | flops 1 | bytes 1 | tf_op jit(solution)/shard_map/part/pallas_call | solution.py:241
  56.1 0.2 collective-permute-done.15.refs_3_
  56.3 2.5 %collective-permute-done.13.refs_1_ = f32[2048,128]{1,0:T(8,128)S(1)} collective-permute-done((f32[2048,128]{1,0:T(8,128)S(1)}, f32[2048,128]{1,0:T(8,128)S(1)}, u32[]{:S(2)}, u32[]{:S(2)}) %collective-permute-start.13) | collective-permute-done | bytes 1048608 | tf_op jit(solution)/shard_map/ppermute | solution.py:41
  58.9 0.1 collective-permute-start.14
  58.9 3.2 %collective-permute-start.16 = (f32[1024,128]{1,0:T(8,128)S(1)}, f32[1024,128]{1,0:T(8,128)S(1)}, u32[]{:S(2)}, u32[]{:S(2)}) collective-permute-start(f32[1024,128]{1,0:T(8,128)S(1)} %slice.15), channel_id=1, source_target_pairs={{0,96},{1,97},{2,98},{3,99},{4,100},{5,101},{6,102},{7,103},{8,104... | collective-permute-start | bytes 1572872 | tf_op jit(solution)/shard_map/ppermute | solution.py:41
  62.2 0.3 collective-permute-start.10
  62.5 0.0 collective-permute-done.11.refs_2_
  62.5 3.1 %collective-permute-start.12 = (f32[1088,128]{1,0:T(8,128)S(1)}, f32[1088,128]{1,0:T(8,128)S(1)}, u32[]{:S(2)}, u32[]{:S(2)}) collective-permute-start(f32[1088,128]{1,0:T(8,128)S(1)} %slice.13), channel_id=1, source_target_pairs={{0,24},{1,25},{2,26},{3,27},{4,28},{5,29},{6,30},{7,31},{8,0},{9,1... | collective-permute-start | bytes 1671176 | tf_op jit(solution)/shard_map/ppermute | solution.py:41
  65.6 5.9 %part.6.refs_2_ = f32[8288,128]{1,0:T(8,128)S(1)} custom-call(s32[352]{0:T(512)S(1)} %select_reduce_fusion.order, s32[11]{0:T(128)S(1)} %convert_reduce_fusion.1.starts, bf16[320,256,128]{2,1,0:T(8,128)(2,1)S(1)} %prepare.1.tiles_ref, f32[2176,128]{1,0:T(8,128)S(1)} %collective-permute-done.9.refs_0_, ...), custom_call_target="tpu_custom_call", output_to_operand_aliasing={{}: (7, {})} | custom-call | flops 1 | bytes 1 | tf_op jit(solution)/shard_map/part/pallas_call | solution.py:241
  71.5 0.6 collective-permute-done.14
  72.1 0.0 collective-permute-done.16
  72.1 0.1 pad_maximum_fusion.refs_0_.refs_1_
  72.1 1.5 %part.7.refs_1_ = f32[8288,128]{1,0:T(8,128)S(1)} custom-call(s32[352]{0:T(512)S(1)} %select_reduce_fusion.order, s32[11]{0:T(128)S(1)} %convert_reduce_fusion.1.starts, bf16[320,256,128]{2,1,0:T(8,128)(2,1)S(1)} %prepare.1.tiles_ref, f32[2048,128]{1,0:T(8,128)S(1)} %pad_maximum_fusion.refs_0_.refs_1_, ...), custom_call_target="tpu_custom_call", output_to_operand_aliasing={{}: (5, {})} | custom-call | flops 1 | bytes 1 | tf_op jit(solution)/shard_map/part/pallas_call | solution.py:241
  73.6 1.9 %collective-permute-done.10 = f32[1088,128]{1,0:T(8,128)S(1)} collective-permute-done((f32[1088,128]{1,0:T(8,128)S(1)}, f32[1088,128]{1,0:T(8,128)S(1)}, u32[]{:S(2)}, u32[]{:S(2)}) %collective-permute-start.10) | collective-permute-done | bytes 557088 | tf_op jit(solution)/shard_map/ppermute | solution.py:41
  75.6 0.0 collective-permute-done.12
  75.6 1.5 %part.8.sums_ref.refs_1_ = f32[8288,128]{1,0:T(8,128)S(1)} custom-call(s32[352]{0:T(512)S(1)} %select_reduce_fusion.order, s32[11]{0:T(128)S(1)} %convert_reduce_fusion.1.starts, bf16[320,256,128]{2,1,0:T(8,128)(2,1)S(1)} %prepare.1.tiles_ref, f32[2176,128]{1,0:T(8,128)S(1)} %constant_dynamic-update-slice_fusion.refs_0_, ...), custom_call_target="tpu_custom_call", output_to_operand_aliasing={{}: (4, {})} | custom-call | flops 1 | bytes 1 | tf_op jit(solution)/shard_map/part/pallas_call | solution.py:241
  77.1 0.1 deal.1
  77.2 0.3 collective-permute-start.17
  77.5 0.5 collective-permute-start.19
  78.0 1.4 %part.9.sums_ref = f32[8288,128]{1,0:T(8,128)S(1)} custom-call(s32[352]{0:T(512)S(1)} %select_reduce_fusion.order, s32[11]{0:T(128)S(1)} %convert_reduce_fusion.1.starts, bf16[320,256,128]{2,1,0:T(8,128)(2,1)S(1)} %prepare.1.tiles_ref, f32[2176,128]{1,0:T(8,128)S(1)} %constant_dynamic-update-slice_fusion.refs_0_, ...), custom_call_target="tpu_custom_call", output_to_operand_aliasing={{}: (4, {})} | custom-call | flops 1 | bytes 1 | tf_op jit(solution)/shard_map/part/pallas_call | solution.py:241
  79.5 0.7 collective-permute-done.17.other_ref
  80.2 0.1 joined.2
  80.3 0.8 collective-permute-start.18
  81.1 0.6 collective-permute-done.19.other_ref
  81.7 0.1 joined.3
  81.8 0.0 copy-start
  81.8 2.0 %collective-permute-start.23 = (f32[512,128]{1,0:T(8,128)S(1)}, f32[512,128]{1,0:T(8,128)S(1)}, u32[]{:S(2)}, u32[]{:S(2)}) collective-permute-start(f32[512,128]{1,0:T(8,128)S(1)} %get-tuple-element.52), channel_id=1, source_target_pairs={{0,6},{1,7},{2,0},{3,1},{4,2},{5,3},{6,4},{7,5},{8,14},{9,15},{10,... | collective-permute-start | bytes 786440 | tf_op jit(solution)/shard_map/ppermute | solution.py:41
  83.8 0.2 collective-permute-start.20
  84.0 6.3 %collective-permute-done.18.passed_ref.refs_2_ = f32[544,128]{1,0:T(8,128)S(1)} collective-permute-done((f32[544,128]{1,0:T(8,128)S(1)}, f32[544,128]{1,0:T(8,128)S(1)}, u32[]{:S(2)}, u32[]{:S(2)}) %collective-permute-start.18) | collective-permute-done | bytes 278560 | tf_op jit(solution)/shard_map/ppermute | solution.py:41
  90.3 0.1 collective-permute-start.21
  90.4 0.3 collective-permute-start.22
  90.7 0.3 collective-permute-done.23.passed_ref
  91.1 3.3 %collective-permute-start.24 = (f32[512,128]{1,0:T(8,128)S(1)}, f32[512,128]{1,0:T(8,128)S(1)}, u32[]{:S(2)}, u32[]{:S(2)}) collective-permute-start(f32[512,128]{1,0:T(8,128)S(1)} %onward.3), channel_id=1, source_target_pairs={{0,6},{1,7},{2,0},{3,1},{4,2},{5,3},{6,4},{7,5},{8,14},{9,15},{10,... | collective-permute-start | bytes 786440 | tf_op jit(solution)/shard_map/ppermute | solution.py:41
  94.3 10.8 %collective-permute-done.22.refs_6_ = f32[512,128]{1,0:T(8,128)S(1)} collective-permute-done((f32[512,128]{1,0:T(8,128)S(1)}, f32[512,128]{1,0:T(8,128)S(1)}, u32[]{:S(2)}, u32[]{:S(2)}) %collective-permute-start.22) | collective-permute-done | bytes 262176 | tf_op jit(solution)/shard_map/ppermute | solution.py:41
  105.1 4.1 %sweep.1 = f32[64,2048]{1,0:T(8,128)} custom-call(f32[64,2048]{1,0:T(8,128)S(1)} %bitcast.5, f32[544,128]{1,0:T(8,128)S(1)} %get-tuple-element.43.refs_1_, f32[544,128]{1,0:T(8,128)S(1)} %collective-permute-done.18.passed_ref.refs_2_, f32[544,128]{1,0:T(8,128)S(1)} %collective-permute-done.20.refs_3_, f32[544,128]{1,0:T(8,128)S(1)} %collective-permute-done.21.refs_4_, ...), custom_call_target="tpu_custom_call" | custom-call | tf_op jit(solution)/shard_map/sweep/pallas_call | solution.py:386
  (22 shorter events, 0.4 us)
Async XLA Ops:
  0.0 4.4 %collective-permute-start = (f32[64,2048]{1,0:T(8,128)}, f32[64,2048]{1,0:T(8,128)S(1)}, u32[]{:S(2)}, u32[]{:S(2)}) collective-permute-start(f32[64,2048]{1,0:T(8,128)} %bitcast.4), channel_id=1, source_target_pairs={{0,0},{1,88},{2,32},{3,120},{4,64},{5,24},{6,96},{7,56},{8,8},{9,8... | collective-permute-start | bytes 1572872 | tf_op jit(solution)/shard_map/ppermute | solution.py:41
  4.4 17.6 %collective-permute-start.5 = (f32[256,128]{1,0:T(8,128)S(1)}, f32[256,128]{1,0:T(8,128)S(1)}, u32[]{:S(2)}, u32[]{:S(2)}) collective-permute-start(f32[256,128]{1,0:T(8,128)S(1)} %get-tuple-element.33.refs_0_), channel_id=1, source_target_pairs={{0,8},{1,9},{2,10},{3,11},{4,12},{5,13},{6,14},{7,15},{8,0},{9,1},... | collective-permute-start | bytes 393224 | tf_op jit(solution)/shard_map/ppermute | solution.py:41
  6.1 18.2 %collective-permute-start.7 = (f32[256,128]{1,0:T(8,128)S(1)}, f32[256,128]{1,0:T(8,128)S(1)}, u32[]{:S(2)}, u32[]{:S(2)}) collective-permute-start(f32[256,128]{1,0:T(8,128)S(1)} %get-tuple-element.34.refs_3_), channel_id=1, source_target_pairs={{0,24},{1,25},{2,26},{3,27},{4,28},{5,29},{6,30},{7,31},{8,16},{9,... | collective-permute-start | bytes 393224 | tf_op jit(solution)/shard_map/ppermute | solution.py:41
  18.6 8.7 %collective-permute-start.3 = (f32[256,128]{1,0:T(8,128)S(1)}, f32[256,128]{1,0:T(8,128)S(1)}, u32[]{:S(2)}, u32[]{:S(2)}) collective-permute-start(f32[256,128]{1,0:T(8,128)S(1)} %get-tuple-element.32.refs_3_), channel_id=1, source_target_pairs={{0,96},{1,97},{2,98},{3,99},{4,100},{5,101},{6,102},{7,103},{8,104... | collective-permute-start | bytes 393224 | tf_op jit(solution)/shard_map/ppermute | solution.py:41
  22.0 5.1 %collective-permute-start.1 = (f32[288,128]{1,0:T(8,128)S(1)}, f32[288,128]{1,0:T(8,128)S(1)}, u32[]{:S(2)}, u32[]{:S(2)}) collective-permute-start(f32[288,128]{1,0:T(8,128)S(1)} %head.1.refs_0_), channel_id=1, source_target_pairs={{0,32},{1,33},{2,34},{3,35},{4,36},{5,37},{6,38},{7,39},{8,40},{9,... | collective-permute-start | bytes 442376 | tf_op jit(solution)/shard_map/ppermute | solution.py:41
  22.0 8.8 %collective-permute-start.6 = (f32[512,128]{1,0:T(8,128)S(1)}, f32[512,128]{1,0:T(8,128)S(1)}, u32[]{:S(2)}, u32[]{:S(2)}) collective-permute-start(f32[512,128]{1,0:T(8,128)S(1)} %pad_maximum_fusion.3), channel_id=1, source_target_pairs={{0,24},{1,25},{2,26},{3,27},{4,28},{5,29},{6,30},{7,31},{8,16},{9,... | collective-permute-start | bytes 786440 | tf_op jit(solution)/shard_map/ppermute | solution.py:41
  24.3 6.5 %collective-permute-start.8 = (f32[512,128]{1,0:T(8,128)S(1)}, f32[512,128]{1,0:T(8,128)S(1)}, u32[]{:S(2)}, u32[]{:S(2)}) collective-permute-start(f32[512,128]{1,0:T(8,128)S(1)} %pad_maximum_fusion.4), channel_id=1, source_target_pairs={{0,8},{1,9},{2,10},{3,11},{4,12},{5,13},{6,14},{7,15},{8,0},{9,1},... | collective-permute-start | bytes 786440 | tf_op jit(solution)/shard_map/ppermute | solution.py:41
  27.2 8.6 %collective-permute-start.2 = (f32[576,128]{1,0:T(8,128)S(1)}, f32[576,128]{1,0:T(8,128)S(1)}, u32[]{:S(2)}, u32[]{:S(2)}) collective-permute-start(f32[576,128]{1,0:T(8,128)S(1)} %pad_maximum_fusion.1), channel_id=1, source_target_pairs={{0,96},{1,97},{2,98},{3,99},{4,100},{5,101},{6,102},{7,103},{8,104... | collective-permute-start | bytes 884744 | tf_op jit(solution)/shard_map/ppermute | solution.py:41
  27.4 8.4 %collective-permute-start.4 = (f32[512,128]{1,0:T(8,128)S(1)}, f32[512,128]{1,0:T(8,128)S(1)}, u32[]{:S(2)}, u32[]{:S(2)}) collective-permute-start(f32[512,128]{1,0:T(8,128)S(1)} %pad_maximum_fusion.2), channel_id=1, source_target_pairs={{0,32},{1,33},{2,34},{3,35},{4,36},{5,37},{6,38},{7,39},{8,40},{9,... | collective-permute-start | bytes 786440 | tf_op jit(solution)/shard_map/ppermute | solution.py:41
  30.9 8.3 %copy-start.1 = (s32[320]{0:T(512)S(1)}, s32[320]{0:T(512)}, u32[]{:S(2)}) copy-start(s32[320]{0:T(512)} %patterns) | copy-start | bytes 3844
  30.9 25.4 %collective-permute-start.15 = (f32[2048,128]{1,0:T(8,128)S(1)}, f32[2048,128]{1,0:T(8,128)S(1)}, u32[]{:S(2)}, u32[]{:S(2)}) collective-permute-start(f32[2048,128]{1,0:T(8,128)S(1)} %laid.3.refs_1_), channel_id=1, source_target_pairs={{0,96},{1,97},{2,98},{3,99},{4,100},{5,101},{6,102},{7,103},{8,104... | collective-permute-start | bytes 3145736 | tf_op jit(solution)/shard_map/ppermute | solution.py:41
  33.5 25.3 %collective-permute-start.13 = (f32[2048,128]{1,0:T(8,128)S(1)}, f32[2048,128]{1,0:T(8,128)S(1)}, u32[]{:S(2)}, u32[]{:S(2)}) collective-permute-start(f32[2048,128]{1,0:T(8,128)S(1)} %laid.3.refs_1_), channel_id=1, source_target_pairs={{0,32},{1,33},{2,34},{3,35},{4,36},{5,37},{6,38},{7,39},{8,40},{9,... | collective-permute-start | bytes 3145736 | tf_op jit(solution)/shard_map/ppermute | solution.py:41
  35.8 26.3 %collective-permute-start.9 = (f32[2176,128]{1,0:T(8,128)S(1)}, f32[2176,128]{1,0:T(8,128)S(1)}, u32[]{:S(2)}, u32[]{:S(2)}) collective-permute-start(f32[2176,128]{1,0:T(8,128)S(1)} %laid.2.refs_0_), channel_id=1, source_target_pairs={{0,8},{1,9},{2,10},{3,11},{4,12},{5,13},{6,14},{7,15},{8,16},{9,17... | collective-permute-start | bytes 3342344 | tf_op jit(solution)/shard_map/ppermute | solution.py:41
  38.0 24.5 %collective-permute-start.11 = (f32[2176,128]{1,0:T(8,128)S(1)}, f32[2176,128]{1,0:T(8,128)S(1)}, u32[]{:S(2)}, u32[]{:S(2)}) collective-permute-start(f32[2176,128]{1,0:T(8,128)S(1)} %laid.2.refs_0_), channel_id=1, source_target_pairs={{0,24},{1,25},{2,26},{3,27},{4,28},{5,29},{6,30},{7,31},{8,0},{9,1... | collective-permute-start | bytes 3342344 | tf_op jit(solution)/shard_map/ppermute | solution.py:41
  58.9 13.2 %collective-permute-start.14 = (f32[1024,128]{1,0:T(8,128)S(1)}, f32[1024,128]{1,0:T(8,128)S(1)}, u32[]{:S(2)}, u32[]{:S(2)}) collective-permute-start(f32[1024,128]{1,0:T(8,128)S(1)} %slice.14), channel_id=1, source_target_pairs={{0,32},{1,33},{2,34},{3,35},{4,36},{5,37},{6,38},{7,39},{8,40},{9,... | collective-permute-start | bytes 1572872 | tf_op jit(solution)/shard_map/ppermute | solution.py:41
  58.9 13.1 %collective-permute-start.16 = (f32[1024,128]{1,0:T(8,128)S(1)}, f32[1024,128]{1,0:T(8,128)S(1)}, u32[]{:S(2)}, u32[]{:S(2)}) collective-permute-start(f32[1024,128]{1,0:T(8,128)S(1)} %slice.15), channel_id=1, source_target_pairs={{0,96},{1,97},{2,98},{3,99},{4,100},{5,101},{6,102},{7,103},{8,104... | collective-permute-start | bytes 1572872 | tf_op jit(solution)/shard_map/ppermute | solution.py:41
  62.2 13.3 %collective-permute-start.10 = (f32[1088,128]{1,0:T(8,128)S(1)}, f32[1088,128]{1,0:T(8,128)S(1)}, u32[]{:S(2)}, u32[]{:S(2)}) collective-permute-start(f32[1088,128]{1,0:T(8,128)S(1)} %slice.12), channel_id=1, source_target_pairs={{0,8},{1,9},{2,10},{3,11},{4,12},{5,13},{6,14},{7,15},{8,16},{9,17... | collective-permute-start | bytes 1671176 | tf_op jit(solution)/shard_map/ppermute | solution.py:41
  62.5 13.1 %collective-permute-start.12 = (f32[1088,128]{1,0:T(8,128)S(1)}, f32[1088,128]{1,0:T(8,128)S(1)}, u32[]{:S(2)}, u32[]{:S(2)}) collective-permute-start(f32[1088,128]{1,0:T(8,128)S(1)} %slice.13), channel_id=1, source_target_pairs={{0,24},{1,25},{2,26},{3,27},{4,28},{5,29},{6,30},{7,31},{8,0},{9,1... | collective-permute-start | bytes 1671176 | tf_op jit(solution)/shard_map/ppermute | solution.py:41
  77.2 2.9 %collective-permute-start.17 = (f32[2080,128]{1,0:T(8,128)S(1)}, f32[2080,128]{1,0:T(8,128)S(1)}, u32[]{:S(2)}, u32[]{:S(2)}) collective-permute-start(f32[2080,128]{1,0:T(8,128)S(1)} %get-tuple-element.40), channel_id=1, source_target_pairs={{0,1},{1,0},{2,3},{3,2},{4,5},{5,4},{6,7},{7,6},{8,9},{9,8},{10,11... | collective-permute-start | bytes 3194888 | tf_op jit(solution)/shard_map/ppermute | solution.py:41
  77.5 4.2 %collective-permute-start.19 = (f32[2048,128]{1,0:T(8,128)S(1)}, f32[2048,128]{1,0:T(8,128)S(1)}, u32[]{:S(2)}, u32[]{:S(2)}) collective-permute-start(f32[2048,128]{1,0:T(8,128)S(1)} %get-tuple-element.41), channel_id=1, source_target_pairs={{0,1},{1,0},{2,3},{3,2},{4,5},{5,4},{6,7},{7,6},{8,9},{9,8},{10,11... | collective-permute-start | bytes 3145736 | tf_op jit(solution)/shard_map/ppermute | solution.py:41
  80.3 10.0 %collective-permute-start.18 = (f32[544,128]{1,0:T(8,128)S(1)}, f32[544,128]{1,0:T(8,128)S(1)}, u32[]{:S(2)}, u32[]{:S(2)}) collective-permute-start(f32[544,128]{1,0:T(8,128)S(1)} %get-tuple-element.44), channel_id=1, source_target_pairs={{0,2},{1,3},{2,4},{3,5},{4,6},{5,7},{6,0},{7,1},{8,10},{9,11},{10,... | collective-permute-start | bytes 835592 | tf_op jit(solution)/shard_map/ppermute | solution.py:41
  81.8 23.3 %copy-start = (f32[2048,64]{0,1:T(8,128)S(1)}, f32[2048,64]{0,1:T(8,128)}, u32[]{:S(2)}) copy-start(f32[2048,64]{0,1:T(8,128)} %param.11) | copy-start | bytes 1572868
  81.8 9.2 %collective-permute-start.23 = (f32[512,128]{1,0:T(8,128)S(1)}, f32[512,128]{1,0:T(8,128)S(1)}, u32[]{:S(2)}, u32[]{:S(2)}) collective-permute-start(f32[512,128]{1,0:T(8,128)S(1)} %get-tuple-element.52), channel_id=1, source_target_pairs={{0,6},{1,7},{2,0},{3,1},{4,2},{5,3},{6,4},{7,5},{8,14},{9,15},{10,... | collective-permute-start | bytes 786440 | tf_op jit(solution)/shard_map/ppermute | solution.py:41
  83.8 21.3 %collective-permute-start.20 = (f32[544,128]{1,0:T(8,128)S(1)}, f32[544,128]{1,0:T(8,128)S(1)}, u32[]{:S(2)}, u32[]{:S(2)}) collective-permute-start(f32[544,128]{1,0:T(8,128)S(1)} %get-tuple-element.48), channel_id=1, source_target_pairs={{0,6},{1,7},{2,0},{3,1},{4,2},{5,3},{6,4},{7,5},{8,14},{9,15},{10,... | collective-permute-start | bytes 835592 | tf_op jit(solution)/shard_map/ppermute | solution.py:41
  90.3 14.8 %collective-permute-start.21 = (f32[544,128]{1,0:T(8,128)S(1)}, f32[544,128]{1,0:T(8,128)S(1)}, u32[]{:S(2)}, u32[]{:S(2)}) collective-permute-start(f32[544,128]{1,0:T(8,128)S(1)} %onward.2), channel_id=1, source_target_pairs={{0,2},{1,3},{2,4},{3,5},{4,6},{5,7},{6,0},{7,1},{8,10},{9,11},{10,... | collective-permute-start | bytes 835592 | tf_op jit(solution)/shard_map/ppermute | solution.py:41
  90.4 14.7 %collective-permute-start.22 = (f32[512,128]{1,0:T(8,128)S(1)}, f32[512,128]{1,0:T(8,128)S(1)}, u32[]{:S(2)}, u32[]{:S(2)}) collective-permute-start(f32[512,128]{1,0:T(8,128)S(1)} %get-tuple-element.50), channel_id=1, source_target_pairs={{0,2},{1,3},{2,4},{3,5},{4,6},{5,7},{6,0},{7,1},{8,10},{9,11},{10,... | collective-permute-start | bytes 786440 | tf_op jit(solution)/shard_map/ppermute | solution.py:41
  91.1 14.1 %collective-permute-start.24 = (f32[512,128]{1,0:T(8,128)S(1)}, f32[512,128]{1,0:T(8,128)S(1)}, u32[]{:S(2)}, u32[]{:S(2)}) collective-permute-start(f32[512,128]{1,0:T(8,128)S(1)} %onward.3), channel_id=1, source_target_pairs={{0,6},{1,7},{2,0},{3,1},{4,2},{5,3},{6,4},{7,5},{8,14},{9,15},{10,... | collective-permute-start | bytes 786440 | tf_op jit(solution)/shard_map/ppermute | solution.py:41
